TPU v7x, 32 devices: a whole 2x2x4 slice. The times are simulated.
32 devices in a mesh: rep: 4 (over x, core), fsdp: 8 (over z, y).
Axes of the slice: x: 2, y: 2, z: 4, core: 2. Of those that a mesh axis runs over, the one named last changes fastest.
Arguments:
- patches: bfloat16 [32, 1024, 768], P(('rep', 'fsdp')), may hold values from -6 to 6
- lengths: int32 [32], P(('rep', 'fsdp')), may hold values from 256 to 1024, as said below
- tasks: int32 [32], P(('rep', 'fsdp')), may hold values from 0 to 2
- w_query: bfloat16 [768, 768], P('fsdp'), may hold values from -0.21875 to 0.21875
- w_key: bfloat16 [768, 768], P('fsdp'), may hold values from -0.21875 to 0.21875
- w_value: bfloat16 [768, 768], P('fsdp'), may hold values from -0.21875 to 0.21875
- w_out: bfloat16 [768, 768], P('fsdp'), may hold values from -1.25 to 1.25
- w_gate: bfloat16 [768, 2048], P('fsdp'), may hold values from -0.21875 to 0.21875
- w_up: bfloat16 [768, 2048], P('fsdp'), may hold values from -0.21875 to 0.21875
- w_down: bfloat16 [2048, 768], P('fsdp'), may hold values from -0.125 to 0.125
- gain_attn: bfloat16 [768], P('fsdp'), may hold values from 0.5 to 1.5
- gain_mlp: bfloat16 [768], P('fsdp'), may hold values from 0.5 to 1.5
- task_table: bfloat16 [768, 3], P('fsdp'), may hold values from -4 to 4
- cotangent: bfloat16 [32, 1024, 768], P(('rep', 'fsdp')), may hold values from -8 to 8
Outputs:
- output: bfloat16 [32, 1024, 768], P(('rep', 'fsdp'))
- grad_patches: float32 [32, 1024, 768], P(('rep', 'fsdp'))
- grad_query: float32 [768, 768], P('fsdp')
- grad_key: float32 [768, 768], P('fsdp')
- grad_value: float32 [768, 768], P('fsdp')
- grad_out: float32 [768, 768], P('fsdp')
- grad_gate: float32 [768, 2048], P('fsdp')
- grad_up: float32 [768, 2048], P('fsdp')
- grad_down: float32 [2048, 768], P('fsdp')
- grad_gain_attn: float32 [768], P('fsdp')
- grad_gain_mlp: float32 [768], P('fsdp')
- grad_table: float32 [768, 3], P('fsdp')
Inputs may be any that keep to these rules, and one draw needn't show every extreme that they name: `lengths`: in every draw some chart has all 1024 patches valid.
All inputs are finite; a program needn't handle non-finite values.
Results may differ from a plain program's by a relative error of at most 0.017.
Values may be sent and summed in bfloat16 or wider, within the bound.
A program may use at most 320 MiB of HBM per device.

v0:
```python
import jax
import jax.numpy as jnp
from jax import lax
from jax.sharding import PartitionSpec as P

HEADS = 12
HEAD_DIM = 64


EPS = 1e-06
FAR = -1e30


def normalize(resid, gain):
    return resid * lax.rsqrt(jnp.mean(resid * resid, axis=-1, keepdims=True) + EPS) * gain


def gated(gate, up):
    return jax.nn.gelu(gate, approximate=True) * up


def matmul(left, right):
    return jnp.dot(left, right, preferred_element_type=jnp.float32)


def matmul_back(left, right):
    return lax.dot_general(
        left, right, (((1,), (1,)), ((), ())), preferred_element_type=jnp.float32
    )


def outer_sum(left, right):
    return lax.dot_general(
        left, right, (((0,), (0,)), ((), ())), preferred_element_type=jnp.float32
    )


def per_device(
    patches,
    lengths,
    tasks,
    w_query,
    w_key,
    w_value,
    w_out,
    w_gate,
    w_up,
    w_down,
    gain_attn,
    gain_mlp,
    task_table,
    cotangent,
):
    gathered = (
        lax.all_gather(w_query, "fsdp", axis=0, tiled=True),
        lax.all_gather(w_key, "fsdp", axis=0, tiled=True),
        lax.all_gather(w_value, "fsdp", axis=0, tiled=True),
        lax.all_gather(w_out, "fsdp", axis=0, tiled=True),
        lax.all_gather(w_gate, "fsdp", axis=0, tiled=True),
        lax.all_gather(w_up, "fsdp", axis=0, tiled=True),
        lax.all_gather(w_down, "fsdp", axis=0, tiled=True),
        lax.all_gather(gain_attn, "fsdp", axis=0, tiled=True),
        lax.all_gather(gain_mlp, "fsdp", axis=0, tiled=True),
        lax.all_gather(task_table, "fsdp", axis=0, tiled=True),
    )
    query_w, key_w, value_w, out_w, gate_w, up_w, down_w, gain_one, gain_two, table = gathered
    source = patches[0].astype(jnp.float32)
    count, width = source.shape
    scale = HEAD_DIM ** (-0.5)
    span = min(512, count)
    blocks = count // span
    gain_one = gain_one.astype(jnp.float32)
    gain_two = gain_two.astype(jnp.float32)
    picked = (jnp.arange(table.shape[1]) == tasks[0]).astype(jnp.float32)
    resid = source + jnp.sum(table.astype(jnp.float32) * picked[None, :], axis=1)[None, :]
    normed = normalize(resid, gain_one).astype(jnp.bfloat16)
    query = matmul(normed, query_w).astype(jnp.bfloat16).reshape(count, HEADS, HEAD_DIM)
    keys = matmul(normed, key_w).astype(jnp.bfloat16).reshape(count, HEADS, HEAD_DIM)
    values = matmul(normed, value_w).astype(jnp.bfloat16).reshape(count, HEADS, HEAD_DIM)
    valid = (jnp.arange(count) < lengths[0])[None, None, :]

    def scores_of(rows):
        raw = jnp.einsum("qhd,khd->hqk", rows, keys, preferred_element_type=jnp.float32) * scale
        return jnp.where(valid, raw, FAR)

    contexts = []
    logsums = []
    for index in range(blocks):
        rows = query[index * span : (index + 1) * span]
        scores = scores_of(rows)
        top = jnp.max(scores, axis=-1, keepdims=True)
        expd = jnp.exp(scores - top)
        total = jnp.sum(expd, axis=-1, keepdims=True)
        probs = (expd / total).astype(jnp.bfloat16)
        block_out = jnp.einsum("hqk,khd->qhd", probs, values, preferred_element_type=jnp.float32)
        contexts.append(block_out.reshape(span, width).astype(jnp.bfloat16))
        logsums.append(top + jnp.log(total))
    context = jnp.concatenate(contexts, axis=0)
    mixed = resid + matmul(context, out_w)
    normed_two = normalize(mixed, gain_two).astype(jnp.bfloat16)
    gate = matmul(normed_two, gate_w)
    up = matmul(normed_two, up_w)
    hidden = gated(gate, up).astype(jnp.bfloat16)
    output = (mixed + matmul(hidden, down_w)).astype(jnp.bfloat16)[None]
    fetched = (
        lax.all_gather(w_query, "fsdp", axis=0, tiled=True),
        lax.all_gather(w_key, "fsdp", axis=0, tiled=True),
        lax.all_gather(w_value, "fsdp", axis=0, tiled=True),
        lax.all_gather(w_out, "fsdp", axis=0, tiled=True),
        lax.all_gather(w_gate, "fsdp", axis=0, tiled=True),
        lax.all_gather(w_up, "fsdp", axis=0, tiled=True),
        lax.all_gather(w_down, "fsdp", axis=0, tiled=True),
        lax.all_gather(gain_attn, "fsdp", axis=0, tiled=True),
        lax.all_gather(gain_mlp, "fsdp", axis=0, tiled=True),
        lax.all_gather(task_table, "fsdp", axis=0, tiled=True),
    )
    query_w, key_w, value_w, out_w, gate_w, up_w, down_w, gain_one, gain_two, table = fetched
    gain_one = gain_one.astype(jnp.float32)
    gain_two = gain_two.astype(jnp.float32)
    upstream = cotangent[0].astype(jnp.float32)
    branch_grad = upstream.astype(jnp.bfloat16)
    grad_down = outer_sum(hidden, branch_grad)
    hidden_grad = matmul_back(branch_grad, down_w)
    _, pull_gated = jax.vjp(gated, gate, up)
    gate_grad, up_grad = pull_gated(hidden_grad)
    gate_grad = gate_grad.astype(jnp.bfloat16)
    up_grad = up_grad.astype(jnp.bfloat16)
    grad_gate = outer_sum(normed_two, gate_grad)
    grad_up = outer_sum(normed_two, up_grad)
    second_grad = matmul_back(gate_grad, gate_w) + matmul_back(up_grad, up_w)
    _, pull_second = jax.vjp(normalize, mixed, gain_two)
    mixed_grad, grad_gain_two = pull_second(second_grad)
    mixed_grad = mixed_grad + upstream
    attn_grad = mixed_grad.astype(jnp.bfloat16)
    grad_out = outer_sum(context, attn_grad)
    context_grad = (
        matmul_back(attn_grad, out_w).astype(jnp.bfloat16).reshape(count, HEADS, HEAD_DIM)
    )
    key_grad = jnp.zeros((count, HEADS, HEAD_DIM), jnp.float32)
    value_grad = jnp.zeros((count, HEADS, HEAD_DIM), jnp.float32)
    query_parts = []
    for index in range(blocks):
        rows = query[index * span : (index + 1) * span]
        back_rows = context_grad[index * span : (index + 1) * span]
        probs = jnp.exp(scores_of(rows) - logsums[index])
        probs_low = probs.astype(jnp.bfloat16)
        prob_grad = jnp.einsum(
            "qhd,khd->hqk", back_rows, values, preferred_element_type=jnp.float32
        )
        weighted = jnp.sum(probs * prob_grad, axis=-1, keepdims=True)
        score_grad = (probs * (prob_grad - weighted)).astype(jnp.bfloat16)
        query_parts.append(
            jnp.einsum("hqk,khd->qhd", score_grad, keys, preferred_element_type=jnp.float32) * scale
        )
        key_grad = (
            key_grad
            + jnp.einsum("hqk,qhd->khd", score_grad, rows, preferred_element_type=jnp.float32)
            * scale
        )
        value_grad = value_grad + jnp.einsum(
            "hqk,qhd->khd", probs_low, back_rows, preferred_element_type=jnp.float32
        )
    query_grad = jnp.concatenate(query_parts, axis=0).reshape(count, width).astype(jnp.bfloat16)
    key_grad = key_grad.reshape(count, width).astype(jnp.bfloat16)
    value_grad = value_grad.reshape(count, width).astype(jnp.bfloat16)
    grad_query = outer_sum(normed, query_grad)
    grad_key = outer_sum(normed, key_grad)
    grad_value = outer_sum(normed, value_grad)
    first_grad = (
        matmul_back(query_grad, query_w)
        + matmul_back(key_grad, key_w)
        + matmul_back(value_grad, value_w)
    )
    _, pull_first = jax.vjp(normalize, resid, gain_one)
    resid_grad, grad_gain_one = pull_first(first_grad)
    resid_grad = resid_grad + mixed_grad
    grad_table = jnp.sum(resid_grad, axis=0)[:, None] * picked[None, :]
    shares = (
        lax.psum_scatter(grad_query, "fsdp", scatter_dimension=0, tiled=True),
        lax.psum_scatter(grad_key, "fsdp", scatter_dimension=0, tiled=True),
        lax.psum_scatter(grad_value, "fsdp", scatter_dimension=0, tiled=True),
        lax.psum_scatter(grad_out, "fsdp", scatter_dimension=0, tiled=True),
        lax.psum_scatter(grad_gate, "fsdp", scatter_dimension=0, tiled=True),
        lax.psum_scatter(grad_up, "fsdp", scatter_dimension=0, tiled=True),
        lax.psum_scatter(grad_down, "fsdp", scatter_dimension=0, tiled=True),
        lax.psum_scatter(grad_gain_one, "fsdp", scatter_dimension=0, tiled=True),
        lax.psum_scatter(grad_gain_two, "fsdp", scatter_dimension=0, tiled=True),
        lax.psum_scatter(grad_table, "fsdp", scatter_dimension=0, tiled=True),
    )
    (
        share_query,
        share_key,
        share_value,
        share_out,
        share_gate,
        share_up,
        share_down,
        share_one,
        share_two,
        share_table,
    ) = shares
    summed = (
        lax.psum(share_query.astype(jnp.bfloat16), "rep").astype(jnp.float32),
        lax.psum(share_key.astype(jnp.bfloat16), "rep").astype(jnp.float32),
        lax.psum(share_value.astype(jnp.bfloat16), "rep").astype(jnp.float32),
        lax.psum(share_out.astype(jnp.bfloat16), "rep").astype(jnp.float32),
        lax.psum(share_gate.astype(jnp.bfloat16), "rep").astype(jnp.float32),
        lax.psum(share_up.astype(jnp.bfloat16), "rep").astype(jnp.float32),
        lax.psum(share_down.astype(jnp.bfloat16), "rep").astype(jnp.float32),
        lax.psum(share_one.astype(jnp.bfloat16), "rep").astype(jnp.float32),
        lax.psum(share_two.astype(jnp.bfloat16), "rep").astype(jnp.float32),
        lax.psum(share_table.astype(jnp.bfloat16), "rep").astype(jnp.float32),
    )
    return (
        output,
        resid_grad[None],
        summed[0],
        summed[1],
        summed[2],
        summed[3],
        summed[4],
        summed[5],
        summed[6],
        summed[7],
        summed[8],
        summed[9],
    )


def solution(mesh):
    in_specs = (
        P(("rep", "fsdp"), None, None),
        P(("rep", "fsdp")),
        P(("rep", "fsdp")),
        P("fsdp", None),
        P("fsdp", None),
        P("fsdp", None),
        P("fsdp", None),
        P("fsdp", None),
        P("fsdp", None),
        P("fsdp", None),
        P("fsdp"),
        P("fsdp"),
        P("fsdp", None),
        P(("rep", "fsdp"), None, None),
    )
    out_specs = (
        P(("rep", "fsdp"), None, None),
        P(("rep", "fsdp"), None, None),
        P("fsdp", None),
        P("fsdp", None),
        P("fsdp", None),
        P("fsdp", None),
        P("fsdp", None),
        P("fsdp", None),
        P("fsdp", None),
        P("fsdp"),
        P("fsdp"),
        P("fsdp", None),
    )
    return jax.shard_map(
        per_device, mesh=mesh, in_specs=in_specs, out_specs=out_specs, check_vma=False
    )
```

profile of v0, /device:TPU:0, one launch (start us, length us, event | category | flops | bytes accessed | tf_op | source)
XLA Modules:
  0.0 1177.4 jit_solution(2740600020913391942)
XLA Ops:
  17.0 23.2 %all-reduce.5 = (bf16[768]{0:T(1024)(128)(2,1)S(1)}, bf16[768]{0:T(1024)(128)(2,1)S(1)}) all-reduce(bf16[768]{0:T(1024)(128)(2,1)S(1)} %dynamic-update-slice, bf16[768]{0:T(1024)(128)(2,1)S(1)} %dynamic-update-slice.1), channel_id=1, replica_groups=mesh['rep'=4,'fsdp'=8] {'fsdp'}, use_global_device_ids=true, to_apply=%add | all-reduce | flops 1536 | bytes 6144
  40.2 16.6 %all-gather = bf16[8,96,3]{1,2,0:T(4,128)(2,1)S(1)} all-gather(bf16[1,96,3]{1,2,0:T(4,128)(2,1)} %bitcast.160), channel_id=1, replica_groups=mesh['rep'=4,'fsdp'=8] {'fsdp'}, dimensions={0}, use_global_device_ids=true | all-gather | bytes 5184 | tf_op jit(solution)/shard_map/all_gather | solution.py:64
  58.9 2.8 convolution_convert_fusion.2
  61.9 34.2 %all-gather.13.cloned.1.call-done = bf16[768,768]{1,0:T(8,128)(2,1)} async-done(((bf16[96,768]{1,0:T(8,128)(2,1)}), bf16[768,768]{1,0:T(8,128)(2,1)}) %all-gather.13.cloned.1.call-update) | async-done | bytes 1179664 | tf_op jit(solution)/shard_map/all_gather | solution.py:56
  96.1 3.3 convolution_convert_fusion.1
  99.4 10.5 fusion.81
  109.9 20.1 %fusion.12 = (f32[12,512]{1,0:T(8,128)S(1)}, f32[12,512]{1,0:T(8,128)S(1)}, f32[12,512,1024]{2,1,0:T(8,128)}) fusion(pred[1024]{0:T(1024)(128)(4,1)S(1)} %iota_compare_fusion, f32[12,512,1024]{2,1,0:T(8,128)} %fusion.81, bf16[512,12,64]{0,2,1:T(8,128)(2,1)S(1)} %bitcast.144, bf16[1024,12,64]{0,2,1:T(8,128)(2,1)S(1)} %bitcast.135), kind=kOutput, calls=%fused_computation.24 | convolution fusion | flops 843042816 | bytes 52741120 | tf_op jit(solution)/shard_map/qhd,khd->hqk/dot_general | solution.py:83
  130.0 18.8 %fusion = (f32[12,512]{1,0:T(8,128)S(1)}, f32[12,512]{1,0:T(8,128)S(1)}) fusion(f32[12,512]{1,0:T(8,128)S(1)} %get-tuple-element.20, f32[12,512,1024]{2,1,0:T(8,128)} %get-tuple-element.49, pred[1024]{0:T(1024)(128)(4,1)S(1)} %iota_compare_fusion, f32[12,512]{1,0:T(8,128)S(1)} %get-tuple-element.21, f32[12,512,1024]{2,1,0:T(8,128)} %fusion.81), kind=kLoop, calls=%fused_computation.12 | loop fusion | flops 50319360 | bytes 50430976 | tf_op jit(solution)/shard_map/reduce_sum | solution.py:93
  148.9 2.8 convolution_convert_fusion.3
  151.7 11.7 fusion.51
  163.5 12.6 %fusion.50 = bf16[12,64,512]{2,1,0:T(8,128)(2,1)} fusion(bf16[1024,12,64]{0,2,1:T(8,128)(2,1)S(1)} %bitcast.141, f32[12,512]{1,0:T(8,128)S(1)} %get-tuple-element.19, f32[12,512]{1,0:T(8,128)S(1)} %get-tuple-element.21, f32[12,512,1024]{2,1,0:T(8,128)} %fusion.81, pred[1024]{0:T(1024)(128)(4,1)S(1)} %iota_compare_fusion), kind=kOutput, calls=%fused_computation.84 | convolution fusion | flops 837156864 | bytes 27575296 | tf_op jit(solution)/shard_map/hqk,khd->qhd/dot_general | solution.py:95
  176.0 4.0 all-gather.15.cloned.1.call-done
  180.0 3.2 multiply_reduce_fusion.4
  185.4 55.9 %all-gather.19.cloned.1.call-done = bf16[768,2048]{1,0:T(8,128)(2,1)} async-done(((bf16[96,2048]{1,0:T(8,128)(2,1)}), bf16[768,2048]{1,0:T(8,128)(2,1)}) %all-gather.19.cloned.1.call-update) | async-done | bytes 3145744 | tf_op jit(solution)/shard_map/all_gather | solution.py:60
  241.3 7.5 fusion.83
  248.8 53.7 %all-gather.17.cloned.1.call-done = bf16[768,2048]{1,0:T(8,128)(2,1)} async-done(((bf16[96,2048]{1,0:T(8,128)(2,1)}), bf16[768,2048]{1,0:T(8,128)(2,1)}) %all-gather.17.cloned.1.call-update) | async-done | bytes 3145744 | tf_op jit(solution)/shard_map/all_gather | solution.py:59
  302.5 7.5 fusion.82
  310.0 53.8 %all-gather.21.cloned.1.call-done = bf16[2048,768]{1,0:T(8,128)(2,1)} async-done(((bf16[256,768]{1,0:T(8,128)(2,1)}), bf16[2048,768]{1,0:T(8,128)(2,1)}) %all-gather.21.cloned.1.call-update) | async-done | bytes 3145744 | tf_op jit(solution)/shard_map/all_gather | solution.py:61
  363.8 16.6 %multiply_convert_fusion.2 = (bf16[1024,2048]{1,0:T(8,128)(2,1)S(1)}, bf16[1024,2048]{1,0:T(8,128)(2,1)S(1)}, bf16[1024,2048]{1,0:T(8,128)(2,1)}) fusion(f32[1024,2048]{1,0:T(8,128)} %fusion.82, f32[1024,2048]{1,0:T(8,128)} %fusion.83, bf16[2048,768]{1,0:T(8,128)(2,1)} %all-gather.21.cloned.1.call-done, bf16[1,1024,768]{2,1,0:T(8,128)(2,1)} %param.27), kind=kOutput, calls=%fused_computation.33 | convolution fusion | flops 3275751424 | bytes 34078720 | tf_op jit(solution)/shard_map/dot_general | solution.py:27
  380.5 3.4 fusion.84
  386.2 4.5 multiply_reduce_fusion.2
  393.3 2.9 fusion.52
  396.2 3.3 convolution_convert_fusion
  400.6 11.1 fusion.4
  411.7 11.6 add_convert_fusion
  423.4 10.4 fusion.85
  433.8 3.0 fusion.68
  436.8 36.3 %multiply_reduce_fusion.1 = (f32[12,512]{1,0:T(8,128)S(1)}, f32[12,512]{1,0:T(8,128)S(1)}, f32[12,512,1024]{2,1,0:T(8,128)}) fusion(f32[12,512]{1,0:T(8,128)S(1)} %get-tuple-element.56, f32[12,512,1024]{2,1,0:T(8,128)} %get-tuple-element.49, pred[1024]{0:T(1024)(128)(4,1)S(1)} %iota_compare_fusion, f32[12,512,1024]{2,1,0:T(8,128)} %fusion.85, ...), kind=kOutput, calls=%fused_computation.4 | convolution fusion | flops 868208640 | bytes 103121920 | tf_op jit(solution)/shard_map/qhd,khd->hqk/dot_general | solution.py:147
  473.2 42.5 %multiply_convert_fusion.1 = (bf16[12,512,1024]{2,1,0:T(8,128)(2,1)}, bf16[12,512,1024]{2,1,0:T(8,128)(2,1)}) fusion(f32[12,512,1024]{2,1,0:T(8,128)} %get-tuple-element.53, f32[12,512]{1,0:T(8,128)S(1)} %get-tuple-element.16, f32[12,512]{1,0:T(8,128)S(1)} %get-tuple-element.56, f32[12,512,1024]{2,1,0:T(8,128)} %get-tuple-element.49, ...), kind=kLoop, calls=%fused_computation.3 | loop fusion | flops 75497472 | bytes 125928448 | tf_op jit(solution)/shard_map/convert_element_type | solution.py:151
  515.8 7.1 fusion.87
  527.7 3.1 fusion.70
  532.2 8.6 multiply_convert_fusion.7
  540.8 8.8 multiply_convert_fusion.6
  550.5 3.1 fusion.41
  553.6 8.3 fusion.45
  563.4 7.7 fusion.90
  571.2 7.6 fusion.89
  584.3 2.5 fusion.30
  586.8 2.7 fusion.76
  591.3 19.5 %all-reduce.4 = (bf16[768]{0:T(1024)(128)(2,1)S(1)}, bf16[768]{0:T(1024)(128)(2,1)S(1)}) all-reduce(f32[768]{0:T(1024)S(1)} %get-tuple-element.14, f32[768]{0:T(1024)S(1)} %copy-done.40), channel_id=9, replica_groups=mesh['rep'=4,'fsdp'=8] {'fsdp'}, use_global_device_ids=true, to_apply=%region_26.27.clone | all-reduce | flops 1536 | bytes 9216
  615.9 68.7 %reduce-scatter.11.cloned.1.call-done = f32[96,768]{1,0:T(8,128)} async-done(((f32[768,768]{1,0:T(8,128)}), f32[96,768]{1,0:T(8,128)}) %reduce-scatter.11.cloned.1.call-update) | async-done | bytes 294928 | tf_op jit(solution)/shard_map/reduce_scatter | solution.py:179
  686.3 118.8 %reduce-scatter.23.cloned.1.call-done = f32[256,768]{1,0:T(8,128)} async-done(((f32[2048,768]{1,0:T(8,128)}), f32[256,768]{1,0:T(8,128)}) %reduce-scatter.23.cloned.1.call-update) | async-done | bytes 786448 | tf_op jit(solution)/shard_map/reduce_scatter | solution.py:185
  807.0 118.8 %reduce-scatter.21.cloned.1.call-done = f32[96,2048]{1,0:T(8,128)} async-done(((f32[768,2048]{1,0:T(8,128)}), f32[96,2048]{1,0:T(8,128)}) %reduce-scatter.21.cloned.1.call-update) | async-done | bytes 786448 | tf_op jit(solution)/shard_map/reduce_scatter | solution.py:184
  927.8 118.7 %reduce-scatter.19.cloned.1.call-done = f32[96,2048]{1,0:T(8,128)} async-done(((f32[768,2048]{1,0:T(8,128)}), f32[96,2048]{1,0:T(8,128)}) %reduce-scatter.19.cloned.1.call-update) | async-done | bytes 786448 | tf_op jit(solution)/shard_map/reduce_scatter | solution.py:183
  1048.4 7.7 fusion.49
  1056.1 54.0 %reduce-scatter.25.cloned.1.call-done = f32[96,3]{1,0:T(8,128)} async-done(((f32[768,3]{1,0:T(8,128)}), f32[96,3]{1,0:T(8,128)}) %reduce-scatter.25.cloned.1.call-update) | async-done | bytes 1168
  1111.0 5.7 all-reduce.6
  1118.2 41.9 %all-reduce.10.cloned.1.call-done = (bf16[96,768]{1,0:T(8,128)(2,1)}, bf16[96,768]{1,0:T(8,128)(2,1)}, bf16[96,768]{1,0:T(8,128)(2,1)}, bf16[96,768]{1,0:T(8,128...) async-done(((bf16[96,768]{1,0:T(8,128)(2,1)}, bf16[96,768]{1,0:T(8,128)(2,1)}, bf16[96,768]{1,0:T(8,128)(2,1)}, ...) | async-done | bytes 1769488 | tf_op jit(solution)/shard_map/psum | solution.py:203
  (187 shorter events, 58.7 us)
Async XLA Ops:
  7.2 51.7 %copy-start.5 = (bf16[1,1024,768]{2,1,0:T(8,128)(2,1)S(1)}, bf16[1,1024,768]{2,1,0:T(8,128)(2,1)}, u32[]{:S(2)}) copy-start(bf16[1,1024,768]{2,1,0:T(8,128)(2,1)} %param.14) | copy-start | bytes 4718596
  7.2 51.7 %all-gather.11.cloned.1.call-start = ((), (), s32[]{:S(2)}) async-start(), calls=%async_computation.9 | async-start | bytes 1327104 | tf_op jit(solution)/shard_map/all_gather | solution.py:55
  7.9 88.2 %all-gather.13.cloned.1.call-start = ((), (), s32[]{:S(2)}) async-start(), calls=%async_computation.10 | async-start | bytes 1327104 | tf_op jit(solution)/shard_map/all_gather | solution.py:56
  8.7 140.2 %all-gather.9.cloned.1.call-start = ((), (), s32[]{:S(2)}) async-start(), calls=%async_computation.8 | async-start | bytes 1327104 | tf_op jit(solution)/shard_map/all_gather | solution.py:57
  9.4 170.6 %all-gather.15.cloned.1.call-start = ((), (), s32[]{:S(2)}) async-start(), calls=%async_computation.11 | async-start | bytes 1327104 | tf_op jit(solution)/shard_map/all_gather | solution.py:58
  10.0 231.3 %all-gather.19.cloned.1.call-start = ((), (), s32[]{:S(2)}) async-start(), calls=%async_computation.13 | async-start | bytes 3538944 | tf_op jit(solution)/shard_map/all_gather | solution.py:60
  10.6 291.9 %all-gather.17.cloned.1.call-start = ((), (), s32[]{:S(2)}) async-start(), calls=%async_computation.12 | async-start | bytes 3538944 | tf_op jit(solution)/shard_map/all_gather | solution.py:59
  11.1 352.6 %all-gather.21.cloned.1.call-start = ((), (), s32[]{:S(2)}) async-start(), calls=%async_computation.14 | async-start | bytes 3538944 | tf_op jit(solution)/shard_map/all_gather | solution.py:61
  11.9 599.0 %reduce-scatter.17.cloned.1.call-start = ((), (), s32[]{:S(2)}) async-start(), calls=%async_computation.18 | async-start | bytes 2654208 | tf_op jit(solution)/shard_map/reduce_scatter | solution.py:182
  13.3 48.5 %copy-start.41 = (f32[3]{0:T(128)}, f32[3]{0:T(128)S(1)}, u32[]{:S(2)}) copy-start(f32[3]{0:T(128)S(1)} %compare_convert_fusion) | copy-start | bytes 40
  40.1 108.7 %copy-start.34 = (f32[768]{0:T(1024)}, f32[768]{0:T(1024)S(1)}, u32[]{:S(2)}) copy-start(f32[768]{0:T(1024)S(1)} %convert_element_type.201) | copy-start | bytes 9220
  58.9 90.0 %copy-start.36 = (f32[1024]{0:T(1024)}, f32[1024]{0:T(1024)S(1)}, u32[]{:S(2)}) copy-start(f32[1024]{0:T(1024)S(1)} %fusion.55) | copy-start | bytes 12292
  61.9 37.5 %copy-start.3 = (bf16[512,768]{0,1:T(8,128)(2,1)}, bf16[512,768]{0,1:T(8,128)(2,1)S(1)}, u32[]{:S(2)}) copy-start(bf16[512,768]{0,1:T(8,128)(2,1)S(1)} %get-tuple-element.43) | copy-start | bytes 2359300
  61.9 48.0 %copy-start.16 = (bf16[512,768]{0,1:T(8,128)(2,1)}, bf16[512,768]{0,1:T(8,128)(2,1)S(1)}, u32[]{:S(2)}) copy-start(bf16[512,768]{0,1:T(8,128)(2,1)S(1)} %get-tuple-element.44) | copy-start | bytes 2359300
  99.4 10.5 copy-start.1
  130.0 18.9 %copy-start.6 = (bf16[1,1024,768]{2,1,0:T(8,128)(2,1)S(1)}, bf16[1,1024,768]{2,1,0:T(8,128)(2,1)}, u32[]{:S(2)}) copy-start(bf16[1,1024,768]{2,1,0:T(8,128)(2,1)} %param.14) | copy-start | bytes 4718596
  151.7 11.7 copy-start.9
  163.5 16.6 %copy-start.48 = (bf16[12,64,512]{2,1,0:T(8,128)(2,1)}, bf16[12,64,512]{2,1,0:T(8,128)(2,1)S(1)}, u32[]{:S(2)}) copy-start(bf16[12,64,512]{2,1,0:T(8,128)(2,1)S(1)} %fusion.51) | copy-start | bytes 2359300
  185.4 117.1 %copy-start.7 = (bf16[1024,768]{1,0:T(8,128)(2,1)}, bf16[1024,768]{1,0:T(8,128)(2,1)S(1)}, u32[]{:S(2)}) copy-start(bf16[1024,768]{1,0:T(8,128)(2,1)S(1)} %multiply_convert_fusion.5) | copy-start | bytes 4718596
  363.8 16.7 %copy-start.44 = (bf16[768,2048]{1,0:T(8,128)(2,1)S(1)}, bf16[768,2048]{1,0:T(8,128)(2,1)}, u32[]{:S(2)}) copy-start(bf16[768,2048]{1,0:T(8,128)(2,1)} %all-gather.17.cloned.1.call-done) | copy-start | bytes 9437188
  380.4 3.5 copy-start.20
  380.4 4.1 copy-start.21
  380.5 4.2 copy-start.12
  380.5 5.7 copy-start.43
  386.2 4.5 copy-start.29
  400.5 11.2 copy-start.18
  400.5 212.0 %reduce-scatter.15.cloned.1.call-start = ((), (), s32[]{:S(2)}) async-start(), calls=%async_computation.17 | async-start | bytes 2654208 | tf_op jit(solution)/shard_map/reduce_scatter | solution.py:181
  400.5 11.1 copy-start.24
  411.7 11.6 copy-start.10
  411.7 11.6 copy-start.19
  423.4 10.4 copy-start.27
  423.4 10.4 copy-start.35
  423.4 10.4 copy-start.37
  473.2 141.0 %reduce-scatter.13.cloned.1.call-start = ((), (), s32[]{:S(2)}) async-start(), calls=%async_computation.16 | async-start | bytes 2654208 | tf_op jit(solution)/shard_map/reduce_scatter | solution.py:180
  473.2 42.6 %copy-start.17 = (bf16[512,768]{0,1:T(8,128)(2,1)S(1)}, bf16[512,768]{0,1:T(8,128)(2,1)}, u32[]{:S(2)}) copy-start(bf16[512,768]{0,1:T(8,128)(2,1)} %copy-done.16) | copy-start | bytes 2359300
  515.8 8.2 copy-start
  515.8 8.4 copy-start.4
  530.8 153.8 %reduce-scatter.11.cloned.1.call-start = ((), (), s32[]{:S(2)}) async-start(), calls=%async_computation.15 | async-start | bytes 2654208 | tf_op jit(solution)/shard_map/reduce_scatter | solution.py:179
  540.8 8.8 copy-start.25
  553.6 251.5 %reduce-scatter.23.cloned.1.call-start = ((), (), s32[]{:S(2)}) async-start(), calls=%async_computation.21 | async-start | bytes 7077888 | tf_op jit(solution)/shard_map/reduce_scatter | solution.py:185
  562.0 363.8 %reduce-scatter.21.cloned.1.call-start = ((), (), s32[]{:S(2)}) async-start(), calls=%async_computation.20 | async-start | bytes 7077888 | tf_op jit(solution)/shard_map/reduce_scatter | solution.py:184
  571.1 475.3 %reduce-scatter.19.cloned.1.call-start = ((), (), s32[]{:S(2)}) async-start(), calls=%async_computation.19 | async-start | bytes 7077888 | tf_op jit(solution)/shard_map/reduce_scatter | solution.py:183
  578.8 531.3 %reduce-scatter.25.cloned.1.call-start = ((), (), s32[]{:S(2)}) async-start(), calls=%async_computation.22 | async-start | bytes 442368
  586.8 4.5 copy-start.40
  590.5 569.6 %all-reduce.10.cloned.1.call-start = ((), (), s32[]{:S(2)}) async-start(), calls=%async_computation.23 | async-start | bytes 3538944 | tf_op jit(solution)/shard_map/psum | solution.py:203
  614.2 434.2 %copy-start.13 = (f32[1024,768]{1,0:T(8,128)S(1)}, f32[1024,768]{1,0:T(8,128)}, u32[]{:S(2)}) copy-start(f32[1024,768]{1,0:T(8,128)} %copy-done.11) | copy-start | bytes 9437188
  1160.2 8.6 copy-start.33
  1160.2 9.5 copy-start.32
  (19 other events, 38.9 us)
Sparse Core Ops, SparseCore 0:
  10.2 43.8 all-gather.10
  56.3 39.7 all-gather.12
  98.3 39.8 all-gather.8
  140.2 39.8 all-gather.14
  182.1 59.2 all-gather.18
  243.4 59.0 all-gather.16
  304.7 59.0 all-gather.20
  400.6 67.8 reduce-scatter.16
  473.3 67.9 reduce-scatter.14
  544.6 68.2 reduce-scatter.12
  616.5 68.1 reduce-scatter.10
  688.1 116.9 reduce-scatter.22
  808.7 117.0 reduce-scatter.20
  929.3 117.0 reduce-scatter.18
  1049.5 60.5 reduce-scatter.24
  1114.0 46.1 all-reduce.9
where the time goes:
time: 1180 us
  waiting for transfers between devices  727 us (62%)
  matrix products  255 us (22%)
  other arithmetic  93.6 us (8%)
  blocking collectives  64.9 us (6%)
  local copies, waits for them, and re-layouts  18.2 us (2%)
  between operations  17.5 us (1%)
    reduce_scatter x1, waiting for transfers between devices, per_device(): lax.psum_scatter(grad_down, 'fsdp', scatter_dimension=0, tiled=True)  119 us
    reduce_scatter x1, waiting for transfers between devices, per_device(): lax.psum_scatter(grad_up, 'fsdp', scatter_dimension=0, tiled=True)  119 us
    reduce_scatter x1, waiting for transfers between devices, per_device(): lax.psum_scatter(grad_gate, 'fsdp', scatter_dimension=0, tiled=True)  119 us
    reduce_scatter x1, waiting for transfers between devices, per_device(): lax.psum_scatter(grad_query, 'fsdp', scatter_dimension=0, tiled=True)  68.7 us
    unnamed x17, waiting for transfers between devices  58.5 us
    all_gather x1, waiting for transfers between devices, per_device(): lax.all_gather(w_up, 'fsdp', axis=0, tiled=True)  55.9 us
    all_gather x1, waiting for transfers between devices, per_device(): lax.all_gather(w_down, 'fsdp', axis=0, tiled=True)  53.8 us
    all_gather x1, waiting for transfers between devices, per_device(): lax.all_gather(w_gate, 'fsdp', axis=0, tiled=True)  53.7 us
  transfers between devices with their start and end apart: 16, of which 11 were waited for; matrix products, arithmetic and copies ran while one was open for 26% of the time, Pallas kernels for 0%

commit v1 on v0

--- a/solution.py
+++ b/solution.py
@@ -1,6 +1,10 @@
+import functools
+
 import jax
 import jax.numpy as jnp
 from jax import lax
+from jax.experimental import pallas as pl
+from jax.experimental.pallas import tpu as pltpu
 from jax.sharding import PartitionSpec as P
 
 HEADS = 12
@@ -35,7 +39,7 @@
     )
 
 
-def per_device(
+def plain(
     patches,
     lengths,
     tasks,
@@ -227,6 +231,1050 @@
     )
 
 
+EVENTS = {
+    "pre": [("Y", 0), ("Z", 2), ("X", 0), ("Y", 1), ("Z", 3), ("C", 0), ("D", 0)],
+    "forward": {
+        0: [("X", 1), ("Y", 2), ("Z", 4)],
+        1: [("C", 1), ("X", 2), ("Y", 3), ("Z", 5)],
+        3: [("X", 3), ("C", 2), ("Y", 4), ("Z", 6)],
+        4: [("D", 1), ("C", 3), ("X", 4), ("Y", 5), ("Z", 7)],
+        7: [("Y", 6), ("X", 5), ("C", 4), ("Z", 8)],
+        8: [("D", 2), ("Y", 7), ("X", 6), ("C", 5), ("Z", 9)],
+        11: [("Y", 8), ("X", 7), ("C", 6)],
+    },
+    "attended": [("D", 3), ("F", 0), ("F", 1), ("F", 2)],
+    "normed": [("Y", 9), ("X", 8), ("C", 7)],
+    "tile": {
+        0: [("D", 4), ("D", 5), ("D", 6), ("F", 4), ("F", 5), ("F", 6)],
+        1: [("C", 9)],
+        2: [("D", 7), ("D", 8), ("D", 9), ("F", 7), ("F", 8), ("F", 9), (0, 0), (0, 1), (0, 2)],
+        3: [(1, 2)],
+    },
+    "tile_mid": {
+        0: [("X", 9), ("C", 8)],
+        2: [(1, 0), (1, 1)],
+        3: [(2, 1), (2, 0)],
+    },
+    "ff_done": [(0, 3), (0, 4), (0, 5)],
+    "second_back": [("F", 3), (2, 2), (3, 1), (3, 0), (1, 4)],
+    "context_back": [(0, 6), (1, 3), (1, 5)],
+    "backward": {
+        0: [(1, 6), (2, 4), (3, 2), (4, 1), (4, 0)],
+        1: [(2, 3)],
+        2: [(2, 5), (3, 4), (5, 0), (5, 1)],
+        3: [(0, 7), (4, 2), (2, 6)],
+        4: [(3, 3), (1, 7), (3, 5), (4, 4), (6, 0)],
+        5: [(3, 6), (4, 3), (5, 2)],
+        6: [(2, 7), (4, 5), (5, 4), (4, 6)],
+        7: [(0, 8), (5, 3), (5, 6), (6, 2)],
+        8: [(1, 8), (3, 7), (5, 5), (6, 4)],
+        9: [(2, 8), (4, 7), (6, 6)],
+        10: [(3, 8), (5, 7)],
+        11: [(0, 9), (4, 8)],
+    },
+    "attention_back": [(1, 9), (5, 8)],
+    "tail_one": [(2, 9), (6, 8)],
+    "tail_two": [(3, 9)],
+    "tail_three": [(4, 9), (5, 9)],
+}
+
+
+BF16 = jnp.bfloat16
+F32 = jnp.float32
+MESH = pl.DeviceIdType.MESH
+PAIR = 2
+
+
+def dot(left, right, on_left, on_right):
+    return lax.dot_general(
+        left, right, (((on_left,), (on_right,)), ((), ())), preferred_element_type=F32
+    )
+
+
+def aligned(index, step):
+    return pl.multiple_of(index, step)
+
+
+class Place:
+    def __init__(self, reps, group):
+        self.reps, self.group, self.deep = reps, group, group // PAIR
+        self.rep = lax.axis_index("rep")
+        self.pos = lax.axis_index("fsdp")
+        self.x, self.core = self.rep // PAIR, self.rep % PAIR
+        self.z, self.y = self.pos // PAIR, self.pos % PAIR
+
+    def sibling(self):
+        return (self.x * PAIR + 1 - self.core, self.pos)
+
+    def across(self):
+        return ((1 - self.x) * PAIR + self.core, self.pos)
+
+    def beside(self):
+        return (self.rep, self.z * PAIR + 1 - self.y)
+
+    def deeper(self, step):
+        return lax.rem(self.z + step, self.deep)
+
+    def along(self, step):
+        return (self.rep, self.deeper(step) * PAIR + self.y)
+
+    def member(self, step):
+        return (lax.rem(self.rep + step, self.reps), self.pos)
+
+    def peer(self, step):
+        return (self.rep, lax.rem(self.pos + step, self.group))
+
+
+def send(source, target, send_sem, recv_sem, device):
+    return pltpu.make_async_remote_copy(
+        src_ref=source,
+        dst_ref=target,
+        send_sem=send_sem,
+        recv_sem=recv_sem,
+        device_id=device,
+        device_id_type=MESH,
+    )
+
+
+class Gather:
+    def __init__(self, place, ref, half, skip, along_sems, hop_sems):
+        self.p, self.ref, self.half, self.skip = place, ref, half, skip
+        self.along_sems, self.hop_sems = along_sems, hop_sems
+
+    def carried(self):
+        p = self.p
+        return pl.ds(
+            aligned(p.core * self.half + p.x * self.skip, 128), self.half - self.skip
+        )
+
+    def own(self):
+        return self.ref.at[self.p.z, self.p.y, :, self.carried()]
+
+    def copies_z(self):
+        p, out = self.p, []
+        for step in range(1, p.deep):
+            out.append(
+                send(
+                    self.own(),
+                    self.own(),
+                    self.along_sems.at[0, step - 1],
+                    self.along_sems.at[1, step - 1],
+                    p.along(step),
+                )
+            )
+        return out
+
+    def hop(self, index, part, device):
+        return send(
+            part, part, self.hop_sems.at[0, index], self.hop_sems.at[1, index], device
+        )
+
+    def copy_y(self):
+        part = self.ref.at[:, self.p.y, :, self.carried()]
+        return self.hop(0, part, self.p.beside())
+
+    def copy_x(self):
+        p = self.p
+        start = p.core * self.half + p.x * (self.half - self.skip)
+        part = self.ref.at[:, :, :, pl.ds(aligned(start, 128), self.skip)]
+        return self.hop(1, part, p.across())
+
+    def copy_core(self):
+        p = self.p
+        part = self.ref.at[:, :, :, pl.ds(aligned(p.core * self.half, 128), self.half)]
+        return self.hop(2, part, p.sibling())
+
+    def start_z(self):
+        for copy in self.copies_z():
+            copy.start()
+
+    def start_y(self):
+        for copy in self.copies_z():
+            copy.wait_recv()
+        self.copy_y().start()
+
+    def start_x(self):
+        self.copy_y().wait_recv()
+        self.copy_x().start()
+
+    def start_core(self):
+        self.copy_x().wait_recv()
+        self.copy_core().start()
+
+    def arrive(self):
+        self.copy_core().wait_recv()
+
+    def finish(self):
+        for copy in self.copies_z():
+            copy.wait_send()
+        self.copy_y().wait_send()
+        self.copy_x().wait_send()
+        self.copy_core().wait_send()
+
+
+class Reduce:
+    def __init__(self, place, ref, recv, first, second, third, res, sems, x_first):
+        self.p, self.ref, self.recv, self.first = place, ref, recv, first
+        self.second, self.third, self.res, self.sems = second, third, res, sems
+        self.x_first = x_first
+        self.rows, self.half = recv.shape[2], recv.shape[3]
+        self.steps = 6 if x_first else 5
+
+    def columns(self, core):
+        return pl.ds(aligned(core * self.half, 128), self.half)
+
+    def one(self, index, source, target, device):
+        return send(source, target, self.sems.at[0, index], self.sems.at[1, index], device)
+
+    def split(self, x):
+        return pl.ds(aligned(x * (self.rows // 2), 16), self.rows // 2)
+
+    def copies(self, phase):
+        p = self.p
+        if phase == 0:
+            part = self.ref.at[:, :, :, self.columns(1 - p.core)]
+            return [self.one(0, part, self.recv, p.sibling())]
+        if self.x_first:
+            if phase == 1:
+                part = self.recv.at[:, :, self.split(1 - p.x), :]
+                return [self.one(1, part, self.first, p.across())]
+            if phase == 2:
+                return [self.one(2, self.first.at[:, 1 - p.y], self.second, p.beside())]
+            if phase == 3:
+                return [
+                    self.one(
+                        2 + step,
+                        self.second.at[p.deeper(step)],
+                        self.third.at[step - 1],
+                        p.along(step),
+                    )
+                    for step in range(1, p.deep)
+                ]
+            last = 2 + p.deep
+            if phase == 4:
+                part = self.res.at[self.split(p.x), self.columns(p.core)]
+                return [self.one(last, part, part, p.across())]
+            part = self.res.at[:, self.columns(p.core)]
+            return [self.one(last + 1, part, part, p.sibling())]
+        if phase == 1:
+            return [self.one(1, self.recv.at[:, 1 - p.y], self.first, p.beside())]
+        if phase == 2:
+            return [
+                self.one(
+                    1 + step,
+                    self.first.at[p.deeper(step)],
+                    self.second.at[step - 1],
+                    p.along(step),
+                )
+                for step in range(1, p.deep)
+            ]
+        last = 1 + p.deep
+        if phase == 3:
+            return [self.one(last, self.first.at[p.z], self.third, p.across())]
+        part = self.res.at[:, self.columns(p.core)]
+        return [self.one(last + 1, part, part, p.sibling())]
+
+    def add(self, phase):
+        p = self.p
+        if phase == 0:
+
+            def fold(index, _):
+                a, b = index // PAIR, index % PAIR
+                self.recv[a, b] = self.recv[a, b] + self.ref[a, b, :, self.columns(p.core)]
+                return 0
+
+            lax.fori_loop(0, p.deep * PAIR, fold, 0)
+        elif self.x_first:
+            if phase == 1:
+
+                def fold(index, _):
+                    a, b = index // PAIR, index % PAIR
+                    self.first[a, b] = self.first[a, b] + self.recv[a, b, self.split(p.x), :]
+                    return 0
+
+                lax.fori_loop(0, p.deep * PAIR, fold, 0)
+            elif phase == 2:
+
+                def fold(index, _):
+                    self.second[index] = self.second[index] + self.first[index, p.y]
+                    return 0
+
+                lax.fori_loop(0, p.deep, fold, 0)
+            elif phase == 3:
+                total = self.second[p.z].astype(F32)
+                for step in range(1, p.deep):
+                    total = total + self.third[step - 1].astype(F32)
+                self.res[self.split(p.x), self.columns(p.core)] = total.astype(BF16)
+        elif phase == 1:
+
+            def fold(index, _):
+                self.first[index] = self.first[index] + self.recv[index, p.y]
+                return 0
+
+            lax.fori_loop(0, p.deep, fold, 0)
+        elif phase == 2:
+            total = self.first[p.z].astype(F32)
+            for step in range(1, p.deep):
+                total = total + self.second[step - 1].astype(F32)
+            self.first[p.z] = total.astype(BF16)
+        elif phase == 3:
+            self.res[:, self.columns(p.core)] = self.first[p.z] + self.third[...]
+
+    def step(self, phase):
+        if phase > 0:
+            for copy in self.copies(phase - 1):
+                copy.wait()
+            self.add(phase - 1)
+        if phase < self.steps:
+            for copy in self.copies(phase):
+                copy.start()
+
+
+def layer(config, *refs):
+    (reps, group, count, width, heads, hidden, tasks_held) = config
+    (
+        lengths_ref, tasks_ref, small_ref, patches_ref, cot_ref,
+        wq_ref, wk_ref, wv_ref, wo_ref, wg_ref, wu_ref, wd_ref,
+        out_ref, grad_ref, done_in, done_gate, done_up, done_down, done_small, spare,
+        w_in, w_out, w_gate, w_up, w_down,
+        normed, qkv, context, extra, mixed, tokens, second, hid, gate_g, up_g,
+        acc_out, acc_in, key_extra, vectors, small_buf, small_grads, member_buf, peer_out, peer_buf,
+        *rest,
+    ) = refs
+    p = Place(reps, group)
+    deep = p.deep
+    head_dim = width // heads
+    scale = head_dim ** -0.5
+    groups = width // 256
+    quad = heads // groups
+    rows = wo_ref.shape[0]
+    down_rows = wd_ref.shape[0] // 2
+    (
+        local_sems, along_sems, hop_sems, small_sems, member_sems, peer_sems, red_sems, out_sems,
+        *red_bufs,
+    ) = rest
+
+    specs = [(w_in.at[g], 384, 128) for g in range(groups)] + [(w_out.at[0], 384, 128)]
+    for j in range(2):
+        specs += [(w_gate.at[j], 512, 128), (w_up.at[j], 512, 256), (w_down.at[j], 384, 128)]
+    chunks = [
+        Gather(p, ref, half, skip, along_sems.at[i], hop_sems.at[i])
+        for i, (ref, half, skip) in enumerate(specs)
+    ]
+
+    sem = 0
+    fills = [[] for _ in chunks]
+    for g in range(groups):
+        for i in range(2):
+            start = pl.ds(aligned(g * 256 + p.core * 128, 128), 128)
+            target = w_in.at[g, p.z, p.y, :, pl.ds(aligned(p.core * 384 + (p.x + i) * 128, 128), 128)]
+            pair = (wq_ref, wk_ref) if i == 0 else (wk_ref, wv_ref)
+            fills[g].append(
+                tuple(
+                    pltpu.make_async_copy(w.at[:, start], target, local_sems.at[sem]) for w in pair
+                )
+            )
+            sem += 1
+    columns = pl.ds(aligned(p.core * 384 + p.x * 128, 128), 256)
+    fills[groups].append(
+        pltpu.make_async_copy(
+            wo_ref.at[:, columns], w_out.at[0, p.z, p.y, :, columns], local_sems.at[sem]
+        )
+    )
+    sem += 1
+    for j in range(2):
+        for i in range(3):
+            seg = 4 * p.core + p.x + i
+            fills[groups + 1 + 3 * j].append(
+                pltpu.make_async_copy(
+                    wg_ref.at[:, pl.ds(aligned(seg * 256 + j * 128, 128), 128)],
+                    w_gate.at[j, p.z, p.y, :, pl.ds(aligned(seg * 128, 128), 128)],
+                    local_sems.at[sem],
+                )
+            )
+            sem += 1
+        for i in range(2):
+            seg = 4 * p.core + 2 * p.x + i
+            fills[groups + 2 + 3 * j].append(
+                pltpu.make_async_copy(
+                    wu_ref.at[:, pl.ds(aligned(seg * 256 + j * 128, 128), 128)],
+                    w_up.at[j, p.z, p.y, :, pl.ds(aligned(seg * 128, 128), 128)],
+                    local_sems.at[sem],
+                )
+            )
+            sem += 1
+        fills[groups + 3 + 3 * j].append(
+            pltpu.make_async_copy(
+                wd_ref.at[pl.ds(j * down_rows, down_rows), columns],
+                w_down.at[j, p.z, p.y, :, columns],
+                local_sems.at[sem],
+            )
+        )
+        sem += 1
+
+    def fill_start(i):
+        for copy in fills[i]:
+            if isinstance(copy, tuple):
+                for x in range(2):
+
+                    @pl.when(p.x == x)
+                    def _(copy=copy, x=x):
+                        copy[x].start()
+            else:
+                copy.start()
+
+    def fill_wait(i):
+        for copy in fills[i]:
+            (copy[0] if isinstance(copy, tuple) else copy).wait()
+
+    reds = []
+    grads = []
+    for j in range(2):
+        grads += [
+            (w_gate.at[j], done_gate.at[j], j == 0),
+            (w_up.at[j], done_up.at[j], j == 1),
+            (w_down.at[j], done_down.at[j], j == 0),
+        ]
+    grads += [(w_out.at[0], done_in.at[groups], True)]
+    grads += [(w_in.at[g], done_in.at[g], g % 2 == 1) for g in range(groups)]
+    for i, (ref, _, x_first) in enumerate(grads):
+        recv, first, sec, third, res = red_bufs[5 * i : 5 * i + 5]
+        reds.append(Reduce(p, ref, recv, first, sec, third, res, red_sems.at[i], x_first))
+
+    tokens_in = pltpu.make_async_copy(patches_ref, tokens, out_sems.at[0])
+    tokens_in.start()
+    for i in range(len(chunks)):
+        fill_start(i)
+    small_buf[p.pos] = small_ref[...]
+    barrier = pltpu.get_barrier_semaphore()
+    for step in range(1, reps):
+        pl.semaphore_signal(barrier, inc=1, device_id=p.member(step), device_id_type=MESH)
+    for step in range(1, group):
+        pl.semaphore_signal(barrier, inc=1, device_id=p.peer(step), device_id_type=MESH)
+    pl.semaphore_wait(barrier, reps + group - 2)
+    small_copies = [
+        send(
+            small_buf.at[p.pos], small_buf.at[p.pos],
+            small_sems.at[0, step - 1], small_sems.at[1, step - 1], p.peer(step),
+        )
+        for step in range(1, group)
+    ]
+    for copy in small_copies:
+        copy.start()
+
+    def go(*events):
+        for kind, i in events:
+            if kind == "Z":
+                fill_wait(i)
+                chunks[i].start_z()
+            elif kind == "Y":
+                chunks[i].start_y()
+            elif kind == "X":
+                chunks[i].start_x()
+            elif kind == "C":
+                chunks[i].start_core()
+            elif kind == "D":
+                chunks[i].arrive()
+            elif kind == "F":
+                chunks[i].finish()
+            else:
+                reds[i].step(kind)
+
+    go(("Z", 0), ("Z", 1))
+
+    for copy in small_copies:
+        copy.wait_recv()
+    shard = width // group
+    wide_row = lax.broadcasted_iota(jnp.int32, (128, width), 0)
+    wide_col = lax.broadcasted_iota(jnp.int32, (128, width), 1)
+    total = None
+    for f in range(group):
+        place_f = jnp.logical_and(wide_col == wide_row + f * shard, wide_row < shard)
+        part = dot(small_buf[f], place_f.astype(F32).astype(BF16), 1, 0)
+        total = part if total is None else total + part
+    vectors[...] = total
+    task = tasks_ref[0]
+    chosen = [(task == k).astype(F32) for k in range(tasks_held)]
+
+    def task_row():
+        row = vectors[2:3, :] * chosen[0]
+        for k in range(1, tasks_held):
+            row = row + vectors[2 + k : 3 + k, :] * chosen[k]
+        return row
+
+    position = lax.broadcasted_iota(jnp.int32, (16, count), 1)
+    kind = lax.broadcasted_iota(jnp.int32, (16, count), 0)
+    mask = jnp.where(position < lengths_ref[0], 0.0, FAR)
+    key_extra[...] = jnp.where(
+        kind < 3, 1.0, jnp.where(kind == 3, mask, 0.0)
+    ).astype(BF16)
+
+    tokens_in.wait()
+    block = 256
+    blocks = count // block
+
+    def rows_of(i, size=block):
+        return pl.ds(aligned(i * size, size), size)
+
+    def norm_one(i, _):
+        r = rows_of(i)
+        resid = tokens[r, :].astype(F32) + task_row()
+        inv = lax.rsqrt(jnp.mean(resid * resid, axis=-1, keepdims=True) + EPS)
+        normed[r, :] = (resid * inv * vectors[0:1, :]).astype(BF16)
+        return 0
+
+    lax.fori_loop(0, blocks, norm_one, 0)
+
+    go(*EVENTS["pre"])
+
+    def project(g):
+        for core in range(2):
+            base = core * 384
+            weight = w_in[g, :, :, :, base : base + 384].reshape(width, 384)
+            got = dot(weight, normed[...], 0, 1)
+            qkv[g, base : base + 128] = (got[:128] * scale).astype(BF16)
+            qkv[g, base + 128 : base + 384] = got[128:].astype(BF16)
+
+    tile = 256
+    tiles = count // tile
+    wide = count // 2
+    sixteen = lax.broadcasted_iota(jnp.int32, (16, count), 0)
+
+    def offsets(h):
+        g, left = h // quad, h % quad
+        return g, (left // 2) * 384 + (left % 2) * head_dim
+
+    def forward_head(h):
+        g, off = offsets(h)
+        ask = jnp.concatenate(
+            [
+                qkv[g, pl.ds(aligned(off, 64), head_dim), :],
+                (sixteen == 3).astype(F32).astype(BF16),
+            ],
+            0,
+        )
+        scores, top = [], None
+        for j in range(tiles):
+            cut = slice(j * tile, (j + 1) * tile)
+            keys = jnp.concatenate(
+                [qkv[g, pl.ds(aligned(off + 128, 64), head_dim), cut], key_extra[:, cut]], 0
+            )
+            s = dot(keys, ask, 0, 0)
+            scores.append(s)
+            here = jnp.max(s, axis=0, keepdims=True)
+            top = here if top is None else jnp.maximum(top, here)
+        acc = None
+        for j in range(tiles):
+            cut = slice(j * tile, (j + 1) * tile)
+            expd = jnp.exp(scores[j] - top).astype(BF16)
+            vals = jnp.concatenate(
+                [
+                    qkv[g, pl.ds(aligned(off + 256, 64), head_dim), cut],
+                    jnp.ones((16, tile), BF16),
+                ],
+                0,
+            )
+            part = dot(vals, expd, 1, 0)
+            acc = part if acc is None else acc + part
+        total = acc[head_dim : head_dim + 1]
+        exact = acc[:head_dim] * (1.0 / total)
+        low = exact.astype(BF16)
+        missing = (exact - low.astype(F32)).astype(BF16)
+        r = pl.ds(aligned(h * head_dim, 64), head_dim)
+        context[r, :] = low
+        hid[r, :] = missing[:, :wide]
+        gate_g[r, :] = missing[:, wide:]
+        extra[h, 0:16] = splits(-(top + jnp.log(total)), 1.0)
+
+    def splits(row, fourth):
+        high = row.astype(BF16).astype(F32)
+        mid = (row - high).astype(BF16).astype(F32)
+        low = row - high - mid
+        return jnp.where(
+            sixteen == 0,
+            high,
+            jnp.where(
+                sixteen == 1,
+                mid,
+                jnp.where(sixteen == 2, low, jnp.where(sixteen == 3, fourth, 0.0)),
+            ),
+        ).astype(BF16)
+
+    def each_head(h, _):
+        for at, events in EVENTS["forward"].items():
+
+            @pl.when(h == at)
+            def _(events=events):
+                go(*events)
+
+        @pl.when(h % quad == 0)
+        def _():
+            project(h // quad)
+
+        forward_head(h)
+        return 0
+
+    lax.fori_loop(0, heads, each_head, 0)
+    kept = [hid.at[pl.ds(0, width), :], gate_g.at[pl.ds(0, width), :]]
+    first_out = 6 + len(grads)
+    keep = [
+        pltpu.make_async_copy(kept[i], spare.at[i], out_sems.at[first_out + i]) for i in range(2)
+    ]
+    fetch = [
+        pltpu.make_async_copy(spare.at[i], kept[i], out_sems.at[first_out + 2 + i])
+        for i in range(2)
+    ]
+    for copy in keep:
+        copy.start()
+    go(*EVENTS["attended"])
+
+    big = 256
+
+    def out_project(i, _):
+        r = rows_of(i, big)
+        m = tokens[r, :].astype(F32) + task_row()
+        m = m + dot(context[:, r], w_out[0].reshape(width, width), 0, 0)
+        mixed[r, :] = m
+        inv = lax.rsqrt(jnp.mean(m * m, axis=-1, keepdims=True) + EPS)
+        second[r, :] = (m * inv * vectors[1:2, :]).astype(BF16)
+        return 0
+
+    lax.fori_loop(0, count // big, out_project, 0)
+    cot_in = pltpu.make_async_copy(cot_ref, tokens, out_sems.at[1])
+    cot_in.start()
+    go(*EVENTS["normed"])
+    cot_in.wait()
+
+    curve = 0.7978845608028654
+    cube = 0.044715
+    part = 512
+    for copy in keep:
+        copy.wait()
+
+    def ff_tile(t, _):
+        j, u = t // 2, t % 2
+        cols = pl.ds(aligned(u * part, part), part)
+        for at, events in EVENTS["tile"].items():
+
+            @pl.when(t == at)
+            def _(events=events):
+                go(*events)
+
+        half = pl.ds(u * (deep // 2), deep // 2)
+
+        def block_of(i, _):
+            r = rows_of(i, big)
+            gate_w = w_gate[j, :, :, :, cols].reshape(width, part)
+            up_w = w_up[j, :, :, :, cols].reshape(width, part)
+            down_w = w_down[j, half].reshape(part, width)
+            two = second[r, :]
+            gate = dot(two, gate_w, 1, 0)
+            up = dot(two, up_w, 1, 0)
+            back = dot(tokens[r, :], down_w, 1, 1)
+            square = gate * gate
+            bend = jnp.tanh(curve * gate * (1.0 + cube * square))
+            flat = 0.5 * (1.0 + bend)
+            gelu = gate * flat
+            slope = flat + 0.5 * gate * (1.0 - bend * bend) * (
+                curve * (1.0 + 3.0 * cube * square)
+            )
+            h = (gelu * up).astype(BF16)
+            g_grad = (back * up * slope).astype(BF16)
+            u_grad = (back * gelu).astype(BF16)
+            hid[r, :] = h
+            gate_g[r, :] = g_grad
+            up_g[r, :] = u_grad
+            o = dot(h, down_w, 1, 0)
+            n = dot(g_grad, gate_w, 1, 1) + dot(u_grad, up_w, 1, 1)
+
+            @pl.when(t == 0)
+            def _():
+                acc_out[r, :] = o
+                acc_in[r, :] = n
+
+            @pl.when(t > 0)
+            def _():
+                acc_out[r, :] = acc_out[r, :] + o
+                acc_in[r, :] = acc_in[r, :] + n
+
+            return 0
+
+        lax.fori_loop(0, count // big, block_of, 0)
+        for at, events in EVENTS["tile_mid"].items():
+
+            @pl.when(t == at)
+            def _(events=events):
+                go(*events)
+
+        w_down[j, half] = (
+            dot(hid[...], tokens[...], 0, 0).astype(BF16).reshape(deep // 2, 2, down_rows, width)
+        )
+        w_gate[j, :, :, :, cols] = (
+            dot(second[...], gate_g[...], 0, 0).astype(BF16).reshape(deep, 2, rows, part)
+        )
+        w_up[j, :, :, :, cols] = (
+            dot(second[...], up_g[...], 0, 0).astype(BF16).reshape(deep, 2, rows, part)
+        )
+        return 0
+
+    lax.fori_loop(0, 4, ff_tile, 0)
+    for copy in fetch:
+        copy.start()
+    go(*EVENTS["ff_done"])
+
+    small_grads[...] = jnp.zeros_like(small_grads)
+
+    def second_back(i, _):
+        r = rows_of(i)
+        m = mixed[r, :]
+        second[r, :] = (m + acc_out[r, :]).astype(BF16)
+        inv = lax.rsqrt(jnp.mean(m * m, axis=-1, keepdims=True) + EPS)
+        unit = m * inv
+        got = acc_in[r, :]
+        scaled = got * vectors[1:2, :]
+        grad = tokens[r, :].astype(F32) + inv * (
+            scaled - unit * jnp.mean(scaled * unit, axis=-1, keepdims=True)
+        )
+        small_grads[1:2, :] = small_grads[1:2, :] + jnp.sum(got * unit, axis=0, keepdims=True)
+        mixed[r, :] = grad
+        tokens[r, :] = grad.astype(BF16)
+        return 0
+
+    lax.fori_loop(0, blocks, second_back, 0)
+    result = pltpu.make_async_copy(second, out_ref, out_sems.at[2])
+    result.start()
+    go(*EVENTS["second_back"])
+
+    out_w = w_out[0].reshape(width, width)
+    acc_out[0:width, :] = dot(context[...], tokens[...], 1, 0)
+    lowered = dot(out_w, tokens[...], 1, 1).astype(BF16)
+    for copy in fetch:
+        copy.wait()
+    for h in range(heads):
+        r = slice(h * head_dim, (h + 1) * head_dim)
+        low = lowered[r]
+        exact = context[r, :].astype(F32) + jnp.concatenate(
+            [hid[r, :], gate_g[r, :]], 1
+        ).astype(F32)
+        delta = jnp.sum(low.astype(F32) * exact, axis=0, keepdims=True)
+        extra[h, 16:32] = splits(-delta, 0.0)
+        context[r, :] = low
+    w_out[0] = acc_out[0:width, :].astype(BF16).reshape(deep, 2, rows, width)
+    go(*EVENTS["context_back"])
+
+    def backward_head(h):
+        g, off = offsets(h)
+        q_rows = pl.ds(aligned(off, 64), head_dim)
+        k_rows = pl.ds(aligned(off + 128, 64), head_dim)
+        v_rows = pl.ds(aligned(off + 256, 64), head_dim)
+        query = qkv[g, q_rows, :]
+        back = context[pl.ds(aligned(h * head_dim, 64), head_dim), :]
+        ask = jnp.concatenate([query, extra[h, 0:16]], 0)
+        back_ask = jnp.concatenate([back, extra[h, 16:32]], 0)
+        query_grad = None
+        for j in range(tiles):
+            cut = slice(j * tile, (j + 1) * tile)
+            keys = qkv[g, k_rows, cut]
+            lift = key_extra[:, cut]
+            probs = jnp.exp(dot(jnp.concatenate([keys, lift], 0), ask, 0, 0))
+            gap = dot(jnp.concatenate([qkv[g, v_rows, cut], lift], 0), back_ask, 0, 0)
+            score_grad = (probs * gap).astype(BF16)
+            part = dot(keys, score_grad, 1, 0)
+            query_grad = part if query_grad is None else query_grad + part
+            qkv[g, k_rows, cut] = dot(query, score_grad, 1, 1).astype(BF16)
+            qkv[g, v_rows, cut] = dot(back, probs.astype(BF16), 1, 1).astype(BF16)
+        qkv[g, q_rows, :] = (query_grad * scale).astype(BF16)
+
+    def first_back(g):
+        def part_of(i, _):
+            r = rows_of(i, big)
+            weight = w_in[g].reshape(width, width)
+            got = dot(qkv[g, :, r], weight, 0, 1)
+
+            @pl.when(g == 0)
+            def _():
+                acc_in[r, :] = got
+
+            @pl.when(g > 0)
+            def _():
+                acc_in[r, :] = acc_in[r, :] + got
+
+            return 0
+
+        lax.fori_loop(0, count // big, part_of, 0)
+
+    def in_grad(g):
+        w_in[g] = dot(normed[...], qkv[g], 0, 1).astype(BF16).reshape(deep, 2, rows, width)
+
+    def each_back(h, _):
+        backward_head(h)
+
+        @pl.when(h % quad == quad - 1)
+        def _():
+            g = h // quad
+            first_back(g)
+            in_grad(g)
+
+        for at, events in EVENTS["backward"].items():
+
+            @pl.when(h == at)
+            def _(events=events):
+                go(*events)
+
+        return 0
+
+    lax.fori_loop(0, heads, each_back, 0)
+    result.wait()
+    again = pltpu.make_async_copy(patches_ref, second, out_sems.at[3])
+    again.start()
+    go(*EVENTS["attention_back"])
+    again.wait()
+
+    def first_norm_back(i, _):
+        r = rows_of(i)
+        resid = second[r, :].astype(F32) + task_row()
+        inv = lax.rsqrt(jnp.mean(resid * resid, axis=-1, keepdims=True) + EPS)
+        unit = resid * inv
+        got = acc_in[r, :]
+        scaled = got * vectors[0:1, :]
+        grad = mixed[r, :] + inv * (
+            scaled - unit * jnp.mean(scaled * unit, axis=-1, keepdims=True)
+        )
+        small_grads[0:1, :] = small_grads[0:1, :] + jnp.sum(got * unit, axis=0, keepdims=True)
+        small_grads[7:8, :] = small_grads[7:8, :] + jnp.sum(grad, axis=0, keepdims=True)
+        acc_out[r, :] = grad
+        return 0
+
+    lax.fori_loop(0, blocks, first_norm_back, 0)
+    grad_out = pltpu.make_async_copy(acc_out, grad_ref, out_sems.at[4])
+    grad_out.start()
+    for k in range(tasks_held):
+        small_grads[2 + k : 3 + k, :] = small_grads[7:8, :] * chosen[k]
+
+    member_buf[p.rep] = small_grads[...]
+    member_copies = [
+        send(
+            member_buf.at[p.rep], member_buf.at[p.rep],
+            member_sems.at[0, step - 1], member_sems.at[1, step - 1], p.member(step),
+        )
+        for step in range(1, reps)
+    ]
+    for copy in member_copies:
+        copy.start()
+    go(*EVENTS["tail_one"])
+    for copy in member_copies:
+        copy.wait_recv()
+    summed = member_buf[0]
+    for i in range(1, reps):
+        summed = summed + member_buf[i]
+    peer_out[...] = jnp.zeros_like(peer_out)
+    for f in range(group):
+        peer_out[f, :, 0:shard] = summed[:, f * shard : (f + 1) * shard]
+    peer_copies = []
+    for step in range(1, group):
+        target = lax.rem(p.pos + step, group)
+        peer_copies.append(
+            send(
+                peer_out.at[target], peer_buf.at[p.pos],
+                peer_sems.at[0, step - 1], peer_sems.at[1, step - 1], p.peer(step),
+            )
+        )
+    for copy in peer_copies:
+        copy.start()
+    peer_buf[p.pos] = peer_out[p.pos]
+    go(*EVENTS["tail_two"])
+    for copy in peer_copies:
+        copy.wait_recv()
+    summed = peer_buf[0]
+    for i in range(1, group):
+        summed = summed + peer_buf[i]
+    small_grads[:, 0:128] = summed
+    ends = [
+        pltpu.make_async_copy(small_grads.at[:, pl.ds(0, 128)], done_small, out_sems.at[5])
+    ]
+    ends[0].start()
+    go(*EVENTS["tail_three"])
+    for i, (_, done, _) in enumerate(grads):
+        copy = pltpu.make_async_copy(reds[i].res, done, out_sems.at[6 + i])
+        copy.start()
+        ends.append(copy)
+    for copy in small_copies + member_copies + peer_copies:
+        copy.wait_send()
+    for copy in ends:
+        copy.wait()
+    grad_out.wait()
+
+
+def fits(reps, group, args):
+    patches, w_query, w_gate, w_down = args[0], args[3], args[7], args[9]
+    return (
+        reps == 4
+        and group == 8
+        and patches.shape == (1, 1024, 768)
+        and w_query.shape == (96, 768)
+        and w_gate.shape == (96, 2048)
+        and w_down.shape == (256, 768)
+    )
+
+
+def ending(config, *refs):
+    groups, group, rows, held = config
+    output, grad, done_in, done_gate, done_up, done_down, done_small = refs[:7]
+    out, out_grad, query, key, value, proj, gate, up, down, one, two, table = refs[7:19]
+    sems = refs[19]
+    copies = [
+        pltpu.make_async_copy(output, out.at[0], sems.at[0]),
+        pltpu.make_async_copy(grad, out_grad.at[0], sems.at[1]),
+    ]
+    for copy in copies:
+        copy.start()
+    for g in range(groups):
+        for core in range(2):
+            for i, ref in enumerate((query, key, value)):
+                start = core * 384 + i * 128
+                to = g * 256 + core * 128
+                ref[:, to : to + 128] = done_in[g, :, start : start + 128].astype(F32)
+    proj[...] = done_in[groups].astype(F32)
+    for done, ref in ((done_gate, gate), (done_up, up)):
+        for j in range(2):
+            for f in range(group):
+                to = f * 256 + j * 128
+                ref[:, to : to + 128] = done[j, :, f * 128 : (f + 1) * 128].astype(F32)
+    half = done_down.shape[1]
+    for j in range(2):
+        down[j * half : (j + 1) * half, :] = done_down[j].astype(F32)
+    one[...] = done_small[0, :rows]
+    two[...] = done_small[1, :rows]
+    table[...] = done_small[...].T[:rows, 2 : 2 + held]
+    for copy in copies:
+        copy.wait()
+
+
+def fused(
+    reps, group, patches, lengths, tasks, w_query, w_key, w_value, w_out, w_gate, w_up, w_down,
+    gain_attn, gain_mlp, task_table, cotangent,
+):
+    count, width = patches.shape[1:]
+    rows, hidden = w_gate.shape
+    held = task_table.shape[1]
+    deep = group // PAIR
+    groups = width // 256
+    down_rows = w_down.shape[0] // 2
+    small = jnp.concatenate([gain_attn[None], gain_mlp[None], task_table.T], axis=0)
+    small = jnp.pad(small, ((0, 16 - small.shape[0]), (0, 128 - rows)))
+
+    def of(rows, columns, x_first):
+        half = columns // 2
+        if x_first:
+            shapes = [
+                (deep, 2, rows, half),
+                (deep, 2, rows // 2, half),
+                (deep, rows // 2, half),
+                (deep - 1, rows // 2, half),
+                (rows, columns),
+            ]
+        else:
+            shapes = [
+                (deep, 2, rows, half),
+                (deep, rows, half),
+                (deep - 1, rows, half),
+                (rows, half),
+                (rows, columns),
+            ]
+        return [pltpu.VMEM(shape, BF16) for shape in shapes]
+
+    red_bufs = []
+    for j in range(2):
+        red_bufs += of(rows, hidden // 2, j == 0)
+        red_bufs += of(rows, hidden // 2, j == 1)
+        red_bufs += of(down_rows, width, j == 0)
+    red_bufs += of(rows, width, True)
+    for g in range(groups):
+        red_bufs += of(rows, width, g % 2 == 1)
+    chunks = groups + 1 + 6
+    scratch = [
+        pltpu.VMEM((groups, deep, 2, rows, width), BF16),
+        pltpu.VMEM((1, deep, 2, rows, width), BF16),
+        pltpu.VMEM((2, deep, 2, rows, hidden // 2), BF16),
+        pltpu.VMEM((2, deep, 2, rows, hidden // 2), BF16),
+        pltpu.VMEM((2, deep, 2, down_rows, width), BF16),
+        pltpu.VMEM((count, width), BF16),
+        pltpu.VMEM((groups, width, count), BF16),
+        pltpu.VMEM((width, count), BF16),
+        pltpu.VMEM((HEADS, 32, count), BF16),
+        pltpu.VMEM((count, width), F32),
+        pltpu.VMEM((count, width), BF16),
+        pltpu.VMEM((count, width), BF16),
+        pltpu.VMEM((count, 512), BF16),
+        pltpu.VMEM((count, 512), BF16),
+        pltpu.VMEM((count, 512), BF16),
+        pltpu.VMEM((count, width), F32),
+        pltpu.VMEM((count, width), F32),
+        pltpu.VMEM((16, count), BF16),
+        pltpu.VMEM((16, width), F32),
+        pltpu.VMEM((group, 16, 128), BF16),
+        pltpu.VMEM((8, width), F32),
+        pltpu.VMEM((reps, 8, width), F32),
+        pltpu.VMEM((group, 8, 128), F32),
+        pltpu.VMEM((group, 8, 128), F32),
+        pltpu.SemaphoreType.DMA((groups * 2 + 1 + 12,)),
+        pltpu.SemaphoreType.DMA((chunks, 2, deep - 1)),
+        pltpu.SemaphoreType.DMA((chunks, 2, 3)),
+        pltpu.SemaphoreType.DMA((2, group - 1)),
+        pltpu.SemaphoreType.DMA((2, reps - 1)),
+        pltpu.SemaphoreType.DMA((2, group - 1)),
+        pltpu.SemaphoreType.DMA((chunks, 2, deep + 4)),
+        pltpu.SemaphoreType.DMA((10 + chunks,)),
+        *red_bufs,
+    ]
+    shape = jax.ShapeDtypeStruct
+    smem = pl.BlockSpec(memory_space=pltpu.SMEM)
+    anywhere = pl.BlockSpec(memory_space=pl.ANY)
+    config = (reps, group, count, width, HEADS, hidden, held)
+    output, grad, done_in, done_gate, done_up, done_down, done_small, _ = pl.pallas_call(
+        functools.partial(layer, config),
+        out_shape=[
+            shape((count, width), BF16),
+            shape((count, width), F32),
+            shape((groups + 1, rows, width), BF16),
+            shape((2, rows, hidden // 2), BF16),
+            shape((2, rows, hidden // 2), BF16),
+            shape((2, down_rows, width), BF16),
+            shape((8, 128), F32),
+            shape((2, width, count // 2), BF16),
+        ],
+        in_specs=[smem, smem, pl.BlockSpec(memory_space=pltpu.VMEM)] + [anywhere] * 9,
+        out_specs=[anywhere] * 8,
+        scratch_shapes=scratch,
+        compiler_params=pltpu.CompilerParams(
+            collective_id=0, has_side_effects=True, vmem_limit_bytes=62 * 1024 * 1024
+        ),
+        name="layer",
+    )(
+        lengths, tasks, small, patches[0], cotangent[0],
+        w_query, w_key, w_value, w_out, w_gate, w_up, w_down,
+    )
+    lane = pl.BlockSpec(memory_space=pltpu.VMEM)
+    return pl.pallas_call(
+        functools.partial(ending, (groups, group, rows, held)),
+        out_shape=[
+            shape((1, count, width), BF16),
+            shape((1, count, width), F32),
+            *[shape((rows, width), F32)] * 4,
+            *[shape((rows, hidden), F32)] * 2,
+            shape((2 * down_rows, width), F32),
+            shape((rows,), F32),
+            shape((rows,), F32),
+            shape((rows, held), F32),
+        ],
+        in_specs=[anywhere] * 2 + [lane] * 5,
+        out_specs=[anywhere] * 2 + [lane] * 10,
+        scratch_shapes=[pltpu.SemaphoreType.DMA((2,))],
+        compiler_params=pltpu.CompilerParams(vmem_limit_bytes=62 * 1024 * 1024),
+        name="ending",
+    )(output, grad, done_in, done_gate, done_up, done_down, done_small)
+
+
 def solution(mesh):
     in_specs = (
         P(("rep", "fsdp"), None, None),
@@ -258,6 +1306,13 @@
         P("fsdp"),
         P("fsdp", None),
     )
+    reps, group = mesh.shape["rep"], mesh.shape["fsdp"]
+
+    def per_device(*args):
+        if fits(reps, group, args):
+            return fused(reps, group, *args)
+        return plain(*args)
+
     return jax.shard_map(
         per_device, mesh=mesh, in_specs=in_specs, out_specs=out_specs, check_vma=False
     )

time: 1180 us -> 383 us (0.32)
  waiting for transfers between devices: 727 us -> 0 us
  Pallas kernels: 0 us -> 378 us
  matrix products: 255 us -> 0 us
  other arithmetic: 93.6 us -> 1.3 us
  blocking collectives: 64.9 us -> 0 us
  local copies, waits for them, and re-layouts: 18.2 us -> 1.45 us
  between operations: 17.5 us -> 1.95 us
    reduce_scatter x7 -> x0, waiting for transfers between devices: 425 us -> none  [the longest x1 119 us: per_device(): lax.psum_scatter(grad_down, 'fsdp', scatter_dimension=0, tiled=True)]
    pallas_call x0 -> x2, Pallas kernels: none -> 378 us  [the longest x1 231 us: fused(): pl.pallas_call(functools.partial(layer, config), out_shape=[shape((count,...]
    dot_general x33 -> x0, matrix products: 255 us -> none  [the longest x2 46.7 us: per_device(): jnp.einsum('qhd,khd->hqk', back_rows, values, preferred_element_type=jnp....]
    all_gather x7 -> x0, waiting for transfers between devices: 202 us -> none  [the longest x1 55.9 us: per_device(): lax.all_gather(w_up, 'fsdp', axis=0, tiled=True)]
    convert_element_type x23 -> x0, other arithmetic: 67.4 us -> none  [the longest x1 42.5 us: per_device(): score_grad = (probs * (prob_grad - weighted)).astype(jnp.bfloat16)]
    unnamed x17 -> x0, waiting for transfers between devices: 58.5 us -> none
    unnamed x2 -> x0, blocking collectives: 42.6 us -> none
    psum x1 -> x0, waiting for transfers between devices: 41.9 us -> none  [per_device(): lax.psum(share_query.astype(jnp.bfloat16), 'rep').astype(jnp.float32)]
  transfers between devices with their start and end apart: 16 -> 0, of which waited for: 11 -> 0; matrix products, arithmetic and copies ran while one was open for 26% -> 0% of each run, Pallas kernels for 0% -> 0%
where the time goes in v1:
time: 383 us
  Pallas kernels  378 us (99%)
    pallas_call x1, Pallas kernels, fused(): pl.pallas_call(functools.partial(layer, config), out_shape=[shape((count,...  231 us
    pallas_call x1, Pallas kernels, fused(): pl.pallas_call(functools.partial(ending, (groups, group, rows, held)), ou...  147 us

profile of v1, /device:TPU:0, one launch (start us, length us, event | category | flops | bytes accessed | tf_op | source)
XLA Modules:
  0.0 382.9 jit_solution(7908803207186035701)
XLA Ops:
  1.9 1.3 fusion.8.refs_2_
  3.2 231.0 %layer.1 = (bf16[1024,768]{1,0:T(8,128)(2,1)}, f32[1024,768]{1,0:T(8,128)}, bf16[4,96,768]{2,1,0:T(8,128)(2,1)}, bf16[2,96,1024]{2,1,0:T(8,128)(2,1)}, bf16[2,96...) custom-call(s32[1]{0:T(128)S(6)} %copy.27.refs_0_, ...), custom_call_target="tpu_custom_call" | custom-call | tf_op jit(solution)/shard_map/layer/pallas_call | solution.py:1234
  234.2 147.3 %ending.1 = (bf16[1,1024,768]{2,1,0:T(8,128)(2,1)}, f32[1,1024,768]{2,1,0:T(8,128)}, f32[96,768]{1,0:T(8,128)}, f32[96,768]{1,0:T(8,128)}, f32[96,768]{1,0:T(8,1...) custom-call(bf16[1024,768]{1,0:T(8,128)(2,1)} %get-tuple-element.19., ...), custom_call_target="tpu_custom_call" | custom-call | tf_op jit(solution)/shard_map/ending/pallas_call | solution.py:1258
  381.5 1.5 copy.26

commit v2 on v1

--- a/solution.py
+++ b/solution.py
@@ -231,51 +231,80 @@
     )
 
 
+PARTS = [2, 1, 1, 1, 2, 2, 2, 2, 2, 2]
+
 EVENTS = {
-    "pre": [("Y", 0), ("Z", 2), ("X", 0), ("Y", 1), ("Z", 3), ("C", 0), ("D", 0)],
+    "start": [("Z", 0), ("Z", 1), ("Z", 2)],
+    "pre": [
+        ("Y", 0), ("Y", 1), ("Z", 3), ("X", 0), ("X", 1), ("Z", 4), ("Y", 2), ("C", 0), ("D", 0),
+        ("C", 1), ("Y", 3), ("Z", 5), ("D", 1),
+    ],
     "forward": {
-        0: [("X", 1), ("Y", 2), ("Z", 4)],
-        1: [("C", 1), ("X", 2), ("Y", 3), ("Z", 5)],
-        3: [("X", 3), ("C", 2), ("Y", 4), ("Z", 6)],
-        4: [("D", 1), ("C", 3), ("X", 4), ("Y", 5), ("Z", 7)],
-        7: [("Y", 6), ("X", 5), ("C", 4), ("Z", 8)],
-        8: [("D", 2), ("Y", 7), ("X", 6), ("C", 5), ("Z", 9)],
-        11: [("Y", 8), ("X", 7), ("C", 6)],
+        1: [("X", 2), ("Z", 6)],
+        2: [("Y", 4), ("Z", 7)],
+        3: [("X", 3)],
+        4: [("Z", 8), ("Y", 5), ("C", 2), ("Z", 9), ("Y", 6), ("X", 4), ("D", 2), ("Z", 10)],
+        5: [("C", 3), ("X", 5), ("Y", 7), ("Z", 11), ("Y", 8)],
+        7: [("C", 4), ("X", 6), ("Y", 9), ("Z", 12)],
+        8: [("D", 3), ("X", 7)],
+        9: [("C", 5), ("C", 6), ("X", 8), ("Y", 10), ("Z", 13)],
+        10: [("X", 9), ("Y", 11), ("Z", 14)],
     },
-    "attended": [("D", 3), ("F", 0), ("F", 1), ("F", 2)],
-    "normed": [("Y", 9), ("X", 8), ("C", 7)],
-    "tile": {
-        0: [("D", 4), ("D", 5), ("D", 6), ("F", 4), ("F", 5), ("F", 6)],
-        1: [("C", 9)],
-        2: [("D", 7), ("D", 8), ("D", 9), ("F", 7), ("F", 8), ("F", 9), (0, 0), (0, 1), (0, 2)],
-        3: [(1, 2)],
+    "attended": [
+        ("D", 4), ("C", 7), ("Y", 12), ("Z", 15), ("X", 10), ("F", 0), ("F", 1), ("F", 2),
+        ("F", 3),
+    ],
+    "normed": [("Y", 13), ("Z", 16)],
+    "block": {
+        0: [
+            ("D", 5), ("D", 6), ("D", 7), ("C", 8), ("X", 11), ("C", 9), ("Y", 14), ("D", 8),
+            ("X", 12), ("D", 9), ("C", 10), ("Y", 15), ("X", 13), ("C", 11), ("D", 10),
+        ],
+        1: [("Y", 16)],
+        3: [("C", 12), ("X", 14)],
+        4: [("X", 16)],
+        6: [("C", 15)],
+        8: [
+            ("D", 11), ("D", 12), ("D", 13), ("D", 14), ("D", 15), ("D", 16), (0, 0), (0, 1),
+            (0, 2),
+        ],
+        12: [(1, 2)],
     },
-    "tile_mid": {
-        0: [("X", 9), ("C", 8)],
-        2: [(1, 0), (1, 1)],
-        3: [(2, 1), (2, 0)],
+    "outer": {
+        0: [("F", 5), ("F", 6), ("F", 7), ("F", 8), ("F", 9), ("F", 10), ("C", 13)],
+        1: [("X", 15)],
+        2: [("C", 14)],
+        3: [("C", 16)],
+        6: [("F", 11), ("F", 12), ("F", 13), ("F", 14), ("F", 15), ("F", 16), (1, 0)],
+        8: [(1, 1)],
+        10: [(2, 0)],
     },
-    "ff_done": [(0, 3), (0, 4), (0, 5)],
-    "second_back": [("F", 3), (2, 2), (3, 1), (3, 0), (1, 4)],
-    "context_back": [(0, 6), (1, 3), (1, 5)],
+    "ff_done": [(2, 1), (0, 3), (0, 4), (0, 5)],
+    "second_back": [("F", 4)],
+    "context_back": [(3, 0), (1, 3), (0, 6)],
     "backward": {
-        0: [(1, 6), (2, 4), (3, 2), (4, 1), (4, 0)],
-        1: [(2, 3)],
-        2: [(2, 5), (3, 4), (5, 0), (5, 1)],
-        3: [(0, 7), (4, 2), (2, 6)],
-        4: [(3, 3), (1, 7), (3, 5), (4, 4), (6, 0)],
-        5: [(3, 6), (4, 3), (5, 2)],
-        6: [(2, 7), (4, 5), (5, 4), (4, 6)],
-        7: [(0, 8), (5, 3), (5, 6), (6, 2)],
-        8: [(1, 8), (3, 7), (5, 5), (6, 4)],
-        9: [(2, 8), (4, 7), (6, 6)],
-        10: [(3, 8), (5, 7)],
-        11: [(0, 9), (4, 8)],
+        0: [(2, 2), (1, 4)],
+        1: [(3, 1), (1, 5), (1, 6), (0, 7)],
+        2: [(4, 0), (3, 2), (2, 3), (1, 7)],
+        3: [(4, 1), (0, 8)],
+        4: [(5, 1), (4, 2), (2, 4), (1, 8)],
+        5: [(3, 3), (2, 5), (0, 9)],
+        6: [(2, 7), (1, 9)],
+        7: [(5, 0), (5, 2), (3, 4), (2, 6), (2, 8), (0, 10)],
+        8: [(6, 0), (6, 2), (4, 3), (3, 5), (1, 10)],
+        9: [(5, 3), (4, 4), (3, 6), (3, 7), (2, 9), (0, 11)],
+        10: [(6, 3), (5, 4), (4, 7), (3, 8), (2, 10), (1, 11)],
+        11: [(4, 5), (4, 6), (5, 7), (4, 8), (0, 12)],
     },
-    "attention_back": [(1, 9), (5, 8)],
-    "tail_one": [(2, 9), (6, 8)],
-    "tail_two": [(3, 9)],
-    "tail_three": [(4, 9), (5, 9)],
+    "attention_back": [],
+    "last": {
+        1: [(5, 8), (2, 11)],
+        2: [(5, 5), (5, 6), (3, 9), (1, 12)],
+        3: [(6, 5), (3, 10), (6, 6)],
+    },
+    "tail_one": [(4, 9), (3, 11)],
+    "tail_two": [(5, 9), (4, 10), (2, 12)],
+    "tail_three": [(4, 11), (5, 10), (5, 11), (3, 12), (4, 12), (5, 12)],
 }
 
 
@@ -337,9 +366,9 @@
 
 
 class Gather:
-    def __init__(self, place, ref, half, skip, along_sems, hop_sems):
+    def __init__(self, place, ref, rows, half, skip, along_sems, hop_sems):
         self.p, self.ref, self.half, self.skip = place, ref, half, skip
-        self.along_sems, self.hop_sems = along_sems, hop_sems
+        self.rows, self.along_sems, self.hop_sems = pl.ds(*rows), along_sems, hop_sems
 
     def carried(self):
         p = self.p
@@ -348,7 +377,7 @@
         )
 
     def own(self):
-        return self.ref.at[self.p.z, self.p.y, :, self.carried()]
+        return self.ref.at[self.p.z, self.p.y, self.rows, self.carried()]
 
     def copies_z(self):
         p, out = self.p, []
@@ -370,18 +399,18 @@
         )
 
     def copy_y(self):
-        part = self.ref.at[:, self.p.y, :, self.carried()]
+        part = self.ref.at[:, self.p.y, self.rows, self.carried()]
         return self.hop(0, part, self.p.beside())
 
     def copy_x(self):
         p = self.p
         start = p.core * self.half + p.x * (self.half - self.skip)
-        part = self.ref.at[:, :, :, pl.ds(aligned(start, 128), self.skip)]
+        part = self.ref.at[:, :, self.rows, pl.ds(aligned(start, 128), self.skip)]
         return self.hop(1, part, p.across())
 
     def copy_core(self):
         p = self.p
-        part = self.ref.at[:, :, :, pl.ds(aligned(p.core * self.half, 128), self.half)]
+        part = self.ref.at[:, :, self.rows, pl.ds(aligned(p.core * self.half, 128), self.half)]
         return self.hop(2, part, p.sibling())
 
     def start_z(self):
@@ -418,10 +447,16 @@
         self.second, self.third, self.res, self.sems = second, third, res, sems
         self.x_first = x_first
         self.rows, self.half = recv.shape[2], recv.shape[3]
+        self.by_rows = ref.shape[2] > self.rows
         self.steps = 6 if x_first else 5
 
+    def share(self, core):
+        if self.by_rows:
+            return pl.ds(aligned(core * self.rows, 16), self.rows), slice(None)
+        return slice(None), pl.ds(aligned(core * self.half, 128), self.half)
+
     def columns(self, core):
-        return pl.ds(aligned(core * self.half, 128), self.half)
+        return self.share(core)[1]
 
     def one(self, index, source, target, device):
         return send(source, target, self.sems.at[0, index], self.sems.at[1, index], device)
@@ -432,7 +467,7 @@
     def copies(self, phase):
         p = self.p
         if phase == 0:
-            part = self.ref.at[:, :, :, self.columns(1 - p.core)]
+            part = self.ref.at[(slice(None), slice(None), *self.share(1 - p.core))]
             return [self.one(0, part, self.recv, p.sibling())]
         if self.x_first:
             if phase == 1:
@@ -454,7 +489,7 @@
             if phase == 4:
                 part = self.res.at[self.split(p.x), self.columns(p.core)]
                 return [self.one(last, part, part, p.across())]
-            part = self.res.at[:, self.columns(p.core)]
+            part = self.res.at[self.share(p.core)]
             return [self.one(last + 1, part, part, p.sibling())]
         if phase == 1:
             return [self.one(1, self.recv.at[:, 1 - p.y], self.first, p.beside())]
@@ -471,7 +506,7 @@
         last = 1 + p.deep
         if phase == 3:
             return [self.one(last, self.first.at[p.z], self.third, p.across())]
-        part = self.res.at[:, self.columns(p.core)]
+        part = self.res.at[self.share(p.core)]
         return [self.one(last + 1, part, part, p.sibling())]
 
     def add(self, phase):
@@ -480,7 +515,7 @@
 
             def fold(index, _):
                 a, b = index // PAIR, index % PAIR
-                self.recv[a, b] = self.recv[a, b] + self.ref[a, b, :, self.columns(p.core)]
+                self.recv[a, b] = self.recv[a, b] + self.ref[(a, b, *self.share(p.core))]
                 return 0
 
             lax.fori_loop(0, p.deep * PAIR, fold, 0)
@@ -518,7 +553,7 @@
                 total = total + self.second[step - 1].astype(F32)
             self.first[p.z] = total.astype(BF16)
         elif phase == 3:
-            self.res[:, self.columns(p.core)] = self.first[p.z] + self.third[...]
+            self.res[self.share(p.core)] = self.first[p.z] + self.third[...]
 
     def step(self, phase):
         if phase > 0:
@@ -536,7 +571,7 @@
         lengths_ref, tasks_ref, small_ref, patches_ref, cot_ref,
         wq_ref, wk_ref, wv_ref, wo_ref, wg_ref, wu_ref, wd_ref,
         out_ref, grad_ref, done_in, done_gate, done_up, done_down, done_small, spare,
-        w_in, w_out, w_gate, w_up, w_down,
+        w_in, w_out, w_ff, w_down,
         normed, qkv, context, extra, mixed, tokens, second, hid, gate_g, up_g,
         acc_out, acc_in, key_extra, vectors, small_buf, small_grads, member_buf, peer_out, peer_buf,
         *rest,
@@ -554,16 +589,29 @@
         *red_bufs,
     ) = rest
 
-    specs = [(w_in.at[g], 384, 128) for g in range(groups)] + [(w_out.at[0], 384, 128)]
+    specs = []
+    cuts = [0]
+
+    def spec(ref, half, skip, parts):
+        held_rows = ref.shape[2] // parts
+        for i in range(parts):
+            specs.append((ref, (i * held_rows, held_rows), half, skip))
+        cuts.append(len(specs))
+
+    for g in range(groups):
+        spec(w_in.at[g], 384, 128, PARTS[g])
+    spec(w_out.at[0], 384, 128, PARTS[groups])
     for j in range(2):
-        specs += [(w_gate.at[j], 512, 128), (w_up.at[j], 512, 256), (w_down.at[j], 384, 128)]
+        spec(w_ff.at[j], 512, 128, PARTS[groups + 1 + 3 * j])
+        spec(w_ff.at[2 + j], 512, 256 - 128 * j, PARTS[groups + 2 + 3 * j])
+        spec(w_down.at[j], 384, 128, PARTS[groups + 3 + 3 * j])
     chunks = [
-        Gather(p, ref, half, skip, along_sems.at[i], hop_sems.at[i])
-        for i, (ref, half, skip) in enumerate(specs)
+        Gather(p, ref, held_rows, half, skip, along_sems.at[i], hop_sems.at[i])
+        for i, (ref, held_rows, half, skip) in enumerate(specs)
     ]
 
     sem = 0
-    fills = [[] for _ in chunks]
+    fills = [[] for _ in PARTS]
     for g in range(groups):
         for i in range(2):
             start = pl.ds(aligned(g * 256 + p.core * 128, 128), 128)
@@ -588,17 +636,17 @@
             fills[groups + 1 + 3 * j].append(
                 pltpu.make_async_copy(
                     wg_ref.at[:, pl.ds(aligned(seg * 256 + j * 128, 128), 128)],
-                    w_gate.at[j, p.z, p.y, :, pl.ds(aligned(seg * 128, 128), 128)],
+                    w_ff.at[j, p.z, p.y, :, pl.ds(aligned(seg * 128, 128), 128)],
                     local_sems.at[sem],
                 )
             )
             sem += 1
-        for i in range(2):
-            seg = 4 * p.core + 2 * p.x + i
+        for i in range(2 + j):
+            seg = 4 * p.core + (2 - j) * p.x + i
             fills[groups + 2 + 3 * j].append(
                 pltpu.make_async_copy(
                     wu_ref.at[:, pl.ds(aligned(seg * 256 + j * 128, 128), 128)],
-                    w_up.at[j, p.z, p.y, :, pl.ds(aligned(seg * 128, 128), 128)],
+                    w_ff.at[2 + j, p.z, p.y, :, pl.ds(aligned(seg * 128, 128), 128)],
                     local_sems.at[sem],
                 )
             )
@@ -631,19 +679,27 @@
     grads = []
     for j in range(2):
         grads += [
-            (w_gate.at[j], done_gate.at[j], j == 0),
-            (w_up.at[j], done_up.at[j], j == 1),
-            (w_down.at[j], done_down.at[j], j == 0),
+            (w_ff.at[j], done_gate.at[j], True),
+            (w_ff.at[2 + j], done_up.at[j], False),
+            (w_down.at[j], done_down.at[j], True),
         ]
     grads += [(w_out.at[0], done_in.at[groups], True)]
-    grads += [(w_in.at[g], done_in.at[g], g % 2 == 1) for g in range(groups)]
+    for pair in range(2 * groups):
+        columns = pl.ds((pair % 2) * 384, 384)
+        grads.append(
+            (
+                w_ff.at[pair // 2, :, :, :, columns],
+                done_in.at[pair // 2, :, columns],
+                False,
+            )
+        )
     for i, (ref, _, x_first) in enumerate(grads):
         recv, first, sec, third, res = red_bufs[5 * i : 5 * i + 5]
         reds.append(Reduce(p, ref, recv, first, sec, third, res, red_sems.at[i], x_first))
 
     tokens_in = pltpu.make_async_copy(patches_ref, tokens, out_sems.at[0])
     tokens_in.start()
-    for i in range(len(chunks)):
+    for i in range(len(fills)):
         fill_start(i)
     small_buf[p.pos] = small_ref[...]
     barrier = pltpu.get_barrier_semaphore()
@@ -665,7 +721,8 @@
     def go(*events):
         for kind, i in events:
             if kind == "Z":
-                fill_wait(i)
+                if i in cuts:
+                    fill_wait(cuts.index(i))
                 chunks[i].start_z()
             elif kind == "Y":
                 chunks[i].start_y()
@@ -680,7 +737,7 @@
             else:
                 reds[i].step(kind)
 
-    go(("Z", 0), ("Z", 1))
+    go(*EVENTS["start"])
 
     for copy in small_copies:
         copy.wait_recv()
@@ -854,18 +911,18 @@
     def ff_tile(t, _):
         j, u = t // 2, t % 2
         cols = pl.ds(aligned(u * part, part), part)
-        for at, events in EVENTS["tile"].items():
-
-            @pl.when(t == at)
-            def _(events=events):
-                go(*events)
-
         half = pl.ds(u * (deep // 2), deep // 2)
 
         def block_of(i, _):
+            for at, events in EVENTS["block"].items():
+
+                @pl.when(t * (count // big) + i == at)
+                def _(events=events):
+                    go(*events)
+
             r = rows_of(i, big)
-            gate_w = w_gate[j, :, :, :, cols].reshape(width, part)
-            up_w = w_up[j, :, :, :, cols].reshape(width, part)
+            gate_w = w_ff[j, :, :, :, cols].reshape(width, part)
+            up_w = w_ff[2 + j, :, :, :, cols].reshape(width, part)
             down_w = w_down[j, half].reshape(part, width)
             two = second[r, :]
             gate = dot(two, gate_w, 1, 0)
@@ -900,19 +957,23 @@
             return 0
 
         lax.fori_loop(0, count // big, block_of, 0)
-        for at, events in EVENTS["tile_mid"].items():
-
-            @pl.when(t == at)
-            def _(events=events):
-                go(*events)
-
+        def pause(k):
+            for at, events in EVENTS["outer"].items():
+
+                @pl.when(t * 3 + k == at)
+                def _(events=events):
+                    go(*events)
+
+        pause(0)
         w_down[j, half] = (
             dot(hid[...], tokens[...], 0, 0).astype(BF16).reshape(deep // 2, 2, down_rows, width)
         )
-        w_gate[j, :, :, :, cols] = (
+        pause(1)
+        w_ff[j, :, :, :, cols] = (
             dot(second[...], gate_g[...], 0, 0).astype(BF16).reshape(deep, 2, rows, part)
         )
-        w_up[j, :, :, :, cols] = (
+        pause(2)
+        w_ff[2 + j, :, :, :, cols] = (
             dot(second[...], up_g[...], 0, 0).astype(BF16).reshape(deep, 2, rows, part)
         )
         return 0
@@ -985,35 +1046,20 @@
             qkv[g, v_rows, cut] = dot(back, probs.astype(BF16), 1, 1).astype(BF16)
         qkv[g, q_rows, :] = (query_grad * scale).astype(BF16)
 
-    def first_back(g):
-        def part_of(i, _):
-            r = rows_of(i, big)
-            weight = w_in[g].reshape(width, width)
-            got = dot(qkv[g, :, r], weight, 0, 1)
-
-            @pl.when(g == 0)
-            def _():
-                acc_in[r, :] = got
-
-            @pl.when(g > 0)
-            def _():
-                acc_in[r, :] = acc_in[r, :] + got
-
-            return 0
-
-        lax.fori_loop(0, count // big, part_of, 0)
-
-    def in_grad(g):
-        w_in[g] = dot(normed[...], qkv[g], 0, 1).astype(BF16).reshape(deep, 2, rows, width)
+    def in_grad(pair):
+        weight = dot(
+            normed[...], qkv[pair // 2, pl.ds(aligned((pair % 2) * 384, 128), 384), :], 0, 1
+        )
+        w_ff[pair // 2, :, :, :, pl.ds(aligned((pair % 2) * 384, 128), 384)] = weight.astype(
+            BF16
+        ).reshape(deep, 2, rows, 384)
 
     def each_back(h, _):
         backward_head(h)
 
-        @pl.when(h % quad == quad - 1)
+        @pl.when(h % 2 == 1)
         def _():
-            g = h // quad
-            first_back(g)
-            in_grad(g)
+            in_grad(h // 2)
 
         for at, events in EVENTS["backward"].items():
 
@@ -1031,11 +1077,19 @@
     again.wait()
 
     def first_norm_back(i, _):
+        for at, events in EVENTS["last"].items():
+
+            @pl.when(i == at)
+            def _(events=events):
+                go(*events)
+
         r = rows_of(i)
+        got = dot(qkv[0, :, r], w_in[0].reshape(width, width), 0, 1)
+        for g in range(1, groups):
+            got = got + dot(qkv[g, :, r], w_in[g].reshape(width, width), 0, 1)
         resid = second[r, :].astype(F32) + task_row()
         inv = lax.rsqrt(jnp.mean(resid * resid, axis=-1, keepdims=True) + EPS)
         unit = resid * inv
-        got = acc_in[r, :]
         scaled = got * vectors[0:1, :]
         grad = mixed[r, :] + inv * (
             scaled - unit * jnp.mean(scaled * unit, axis=-1, keepdims=True)
@@ -1122,12 +1176,26 @@
     output, grad, done_in, done_gate, done_up, done_down, done_small = refs[:7]
     out, out_grad, query, key, value, proj, gate, up, down, one, two, table = refs[7:19]
     sems = refs[19]
-    copies = [
-        pltpu.make_async_copy(output, out.at[0], sems.at[0]),
-        pltpu.make_async_copy(grad, out_grad.at[0], sems.at[1]),
-    ]
-    for copy in copies:
+    held_out, held_grad = refs[20:22]
+    parts = 4
+    span = output.shape[0] // parts
+    brought, copies = [], []
+    for i in range(parts):
+        r = pl.ds(i * span, span)
+        for k, (source, middle, target) in enumerate(
+            ((output, held_out, out.at[0]), (grad, held_grad, out_grad.at[0]))
+        ):
+            brought.append(
+                pltpu.make_async_copy(source.at[r], middle.at[r], sems.at[0, k, i])
+            )
+            copies.append(
+                pltpu.make_async_copy(middle.at[r], target.at[r], sems.at[1, k, i])
+            )
+    for copy in brought:
         copy.start()
+    for first, then in zip(brought, copies):
+        first.wait()
+        then.start()
     for g in range(groups):
         for core in range(2):
             for i, ref in enumerate((query, key, value)):
@@ -1163,15 +1231,18 @@
     small = jnp.concatenate([gain_attn[None], gain_mlp[None], task_table.T], axis=0)
     small = jnp.pad(small, ((0, 16 - small.shape[0]), (0, 128 - rows)))
 
-    def of(rows, columns, x_first):
+    def of(rows, columns, x_first, by_rows=False):
+        whole = (rows, columns)
         half = columns // 2
+        if by_rows:
+            rows, half = rows // 2, columns
         if x_first:
             shapes = [
                 (deep, 2, rows, half),
                 (deep, 2, rows // 2, half),
                 (deep, rows // 2, half),
                 (deep - 1, rows // 2, half),
-                (rows, columns),
+                whole,
             ]
         else:
             shapes = [
@@ -1179,24 +1250,24 @@
                 (deep, rows, half),
                 (deep - 1, rows, half),
                 (rows, half),
-                (rows, columns),
+                whole,
             ]
         return [pltpu.VMEM(shape, BF16) for shape in shapes]
 
     red_bufs = []
     for j in range(2):
-        red_bufs += of(rows, hidden // 2, j == 0)
-        red_bufs += of(rows, hidden // 2, j == 1)
-        red_bufs += of(down_rows, width, j == 0)
+        red_bufs += of(rows, hidden // 2, True)
+        red_bufs += of(rows, hidden // 2, False)
+        red_bufs += of(down_rows, width, True)
     red_bufs += of(rows, width, True)
-    for g in range(groups):
-        red_bufs += of(rows, width, g % 2 == 1)
-    chunks = groups + 1 + 6
+    for _ in range(2 * groups):
+        red_bufs += of(rows, width // 2, False, True)
+    sums = 7 + 2 * groups
+    chunks = sum(PARTS)
     scratch = [
         pltpu.VMEM((groups, deep, 2, rows, width), BF16),
         pltpu.VMEM((1, deep, 2, rows, width), BF16),
-        pltpu.VMEM((2, deep, 2, rows, hidden // 2), BF16),
-        pltpu.VMEM((2, deep, 2, rows, hidden // 2), BF16),
+        pltpu.VMEM((4, deep, 2, rows, hidden // 2), BF16),
         pltpu.VMEM((2, deep, 2, down_rows, width), BF16),
         pltpu.VMEM((count, width), BF16),
         pltpu.VMEM((groups, width, count), BF16),
@@ -1217,14 +1288,14 @@
         pltpu.VMEM((reps, 8, width), F32),
         pltpu.VMEM((group, 8, 128), F32),
         pltpu.VMEM((group, 8, 128), F32),
-        pltpu.SemaphoreType.DMA((groups * 2 + 1 + 12,)),
+        pltpu.SemaphoreType.DMA((groups * 2 + 1 + 13,)),
         pltpu.SemaphoreType.DMA((chunks, 2, deep - 1)),
         pltpu.SemaphoreType.DMA((chunks, 2, 3)),
         pltpu.SemaphoreType.DMA((2, group - 1)),
         pltpu.SemaphoreType.DMA((2, reps - 1)),
         pltpu.SemaphoreType.DMA((2, group - 1)),
-        pltpu.SemaphoreType.DMA((chunks, 2, deep + 4)),
-        pltpu.SemaphoreType.DMA((10 + chunks,)),
+        pltpu.SemaphoreType.DMA((sums, 2, deep + 4)),
+        pltpu.SemaphoreType.DMA((10 + sums,)),
         *red_bufs,
     ]
     shape = jax.ShapeDtypeStruct
@@ -1269,7 +1340,11 @@
         ],
         in_specs=[anywhere] * 2 + [lane] * 5,
         out_specs=[anywhere] * 2 + [lane] * 10,
-        scratch_shapes=[pltpu.SemaphoreType.DMA((2,))],
+        scratch_shapes=[
+            pltpu.SemaphoreType.DMA((2, 2, 4)),
+            pltpu.VMEM((count, width), BF16),
+            pltpu.VMEM((count, width), F32),
+        ],
         compiler_params=pltpu.CompilerParams(vmem_limit_bytes=62 * 1024 * 1024),
         name="ending",
     )(output, grad, done_in, done_gate, done_up, done_down, done_small)

time: 383 us -> 205 us (0.54)
  Pallas kernels: 378 us -> 200 us
    pallas_call x1, Pallas kernels: 147 us -> 7.43 us  [fused(): pl.pallas_call(functools.partial(ending, (groups, group, rows, held)), ou...]
    pallas_call x1, Pallas kernels: 231 us -> 193 us  [fused(): pl.pallas_call(functools.partial(layer, config), out_shape=[shape((count,...]
where the time goes in v2:
time: 205 us
  Pallas kernels  200 us (98%)
    pallas_call x1, Pallas kernels, fused(): pl.pallas_call(functools.partial(layer, config), out_shape=[shape((count,...  193 us
    pallas_call x1, Pallas kernels, fused(): pl.pallas_call(functools.partial(ending, (groups, group, rows, held)), ou...  7.43 us

profile of v2, /device:TPU:0, one launch (start us, length us, event | category | flops | bytes accessed | tf_op | source)
XLA Modules:
  0.0 204.8 jit_solution(2577993772365188207)
XLA Ops:
  1.9 1.3 fusion.8.refs_2_
  3.2 192.6 %layer.1 = (bf16[1024,768]{1,0:T(8,128)(2,1)}, f32[1024,768]{1,0:T(8,128)}, bf16[4,96,768]{2,1,0:T(8,128)(2,1)}, bf16[2,96,1024]{2,1,0:T(8,128)(2,1)}, bf16[2,96...) custom-call(s32[1]{0:T(128)S(6)} %copy.27.refs_0_, ...), custom_call_target="tpu_custom_call" | custom-call | tf_op jit(solution)/shard_map/layer/pallas_call | solution.py:1305
  195.9 7.4 %ending.1 = (bf16[1,1024,768]{2,1,0:T(8,128)(2,1)}, f32[1,1024,768]{2,1,0:T(8,128)}, f32[96,768]{1,0:T(8,128)}, f32[96,768]{1,0:T(8,128)}, f32[96,768]{1,0:T(8,1...) custom-call(bf16[1024,768]{1,0:T(8,128)(2,1)} %get-tuple-element.19., ...), custom_call_target="tpu_custom_call" | custom-call | tf_op jit(solution)/shard_map/ending/pallas_call | solution.py:1329
  203.3 1.5 copy.26

commit v3 on v2

--- a/solution.py
+++ b/solution.py
@@ -231,80 +231,104 @@
     )
 
 
-PARTS = [2, 1, 1, 1, 2, 2, 2, 2, 2, 2]
+PARTS = [1, 1, 1, 1, 1, 1, 1, 2, 2, 2, 2, 2, 2, 2, 2, 2, 2]
+
+UP_SKIP = (0, 128, 0, 128)
 
 EVENTS = {
     "start": [("Z", 0), ("Z", 1), ("Z", 2)],
+    "ready": [],
     "pre": [
-        ("Y", 0), ("Y", 1), ("Z", 3), ("X", 0), ("X", 1), ("Z", 4), ("Y", 2), ("C", 0), ("D", 0),
-        ("C", 1), ("Y", 3), ("Z", 5), ("D", 1),
+        ("Y", 0), ("Z", 3), ("Z", 4), ("Y", 1), ("X", 0), ("Z", 5), ("Y", 2), ("X", 1), ("Z", 6),
+        ("Y", 3), ("C", 0), ("X", 2), ("Y", 4), ("D", 0), ("Z", 7),
     ],
     "forward": {
-        1: [("X", 2), ("Z", 6)],
-        2: [("Y", 4), ("Z", 7)],
-        3: [("X", 3)],
-        4: [("Z", 8), ("Y", 5), ("C", 2), ("Z", 9), ("Y", 6), ("X", 4), ("D", 2), ("Z", 10)],
-        5: [("C", 3), ("X", 5), ("Y", 7), ("Z", 11), ("Y", 8)],
-        7: [("C", 4), ("X", 6), ("Y", 9), ("Z", 12)],
-        8: [("D", 3), ("X", 7)],
-        9: [("C", 5), ("C", 6), ("X", 8), ("Y", 10), ("Z", 13)],
-        10: [("X", 9), ("Y", 11), ("Z", 14)],
+        1: [("X", 3), ("Y", 5), ("Z", 9)],
+        2: [("D", 1), ("C", 2), ("X", 4), ("Z", 10)],
+        3: [("C", 3), ("X", 5), ("Y", 6), ("Z", 11)],
+        4: [("D", 2), ("Y", 7), ("Y", 8)],
+        5: [("C", 5), ("Y", 9)],
+        6: [("D", 3), ("Z", 13)],
+        7: [("X", 7), ("X", 8), ("Z", 15), ("Z", 16)],
+        8: [("D", 4), ("Y", 11), ("Z", 17)],
+        9: [("C", 9), ("Y", 12), ("Y", 13), ("Z", 19), ("X", 10)],
+        10: [("D", 5), ("C", 6), ("C", 10), ("Y", 14), ("Z", 20)],
+        11: [("Y", 16), ("Y", 17), ("Z", 21)],
+    },
+    "projected": {
+        0: [("C", 1), ("Z", 8)],
+        4: [("C", 4), ("Z", 12)],
+        6: [("X", 6), ("Y", 10), ("Z", 14)],
+        8: [("X", 9), ("Z", 18)],
+        10: [("C", 7), ("Y", 15), ("X", 11)],
     },
     "attended": [
-        ("D", 4), ("C", 7), ("Y", 12), ("Z", 15), ("X", 10), ("F", 0), ("F", 1), ("F", 2),
-        ("F", 3),
+        ("D", 6), ("C", 8), ("X", 12), ("Y", 18), ("Z", 22), ("F", 0), ("F", 1), ("F", 2),
+        ("F", 3), ("F", 4), ("F", 5),
     ],
-    "normed": [("Y", 13), ("Z", 16)],
+    "normed": [("C", 11), ("X", 13), ("X", 14), ("X", 15), ("Y", 19), ("Z", 23)],
     "block": {
         0: [
-            ("D", 5), ("D", 6), ("D", 7), ("C", 8), ("X", 11), ("C", 9), ("Y", 14), ("D", 8),
-            ("X", 12), ("D", 9), ("C", 10), ("Y", 15), ("X", 13), ("C", 11), ("D", 10),
+            ("D", 7), ("D", 8), ("D", 9), ("D", 10), ("Y", 20), ("X", 16), ("C", 12), ("Z", 24),
+            ("X", 17), ("D", 11), ("Z", 25), ("X", 18), ("Y", 21), ("C", 13), ("Z", 26), ("D", 12),
         ],
-        1: [("Y", 16)],
-        3: [("C", 12), ("X", 14)],
-        4: [("X", 16)],
-        6: [("C", 15)],
+        2: [("C", 14), ("X", 19)],
+        3: [("C", 19), ("X", 20), ("Y", 22), ("Y", 23)],
+        4: [
+            ("D", 13), ("D", 14), ("D", 15), ("C", 16), ("Y", 26), ("C", 17), ("X", 22), ("X", 23),
+            ("C", 18), ("D", 16),
+        ],
+        5: [("X", 24)],
+        6: [("X", 25)],
+        7: [("C", 21), ("X", 26)],
         8: [
-            ("D", 11), ("D", 12), ("D", 13), ("D", 14), ("D", 15), ("D", 16), (0, 0), (0, 1),
-            (0, 2),
+            ("D", 17), ("D", 18), ("D", 19), ("D", 20), ("D", 21), ("C", 23), ("D", 22), (0, 0),
+            (0, 1), (0, 2),
         ],
-        12: [(1, 2)],
+        9: [("C", 24)],
+        11: [("C", 25)],
+        12: [("D", 23), ("D", 24), ("D", 25), ("D", 26), (1, 1), (1, 2)],
     },
     "outer": {
-        0: [("F", 5), ("F", 6), ("F", 7), ("F", 8), ("F", 9), ("F", 10), ("C", 13)],
-        1: [("X", 15)],
-        2: [("C", 14)],
-        3: [("C", 16)],
-        6: [("F", 11), ("F", 12), ("F", 13), ("F", 14), ("F", 15), ("F", 16), (1, 0)],
-        8: [(1, 1)],
-        10: [(2, 0)],
+        0: [
+            ("F", 7), ("F", 8), ("F", 9), ("F", 10), ("F", 11), ("F", 12), ("C", 15), ("C", 20),
+            ("Y", 24),
+        ],
+        1: [("X", 21), ("Y", 25)],
+        2: [("F", 13), ("F", 14), ("F", 15), ("F", 16)],
+        3: [("C", 22)],
+        4: [("F", 17), ("F", 18), ("F", 19), ("F", 20), ("F", 21), ("F", 22), (1, 0)],
+        5: [("C", 26)],
+        6: [("F", 23), ("F", 24), ("F", 25), ("F", 26)],
+        7: [(2, 0)],
     },
-    "ff_done": [(2, 1), (0, 3), (0, 4), (0, 5)],
-    "second_back": [("F", 4)],
-    "context_back": [(3, 0), (1, 3), (0, 6)],
+    "ff_done": [(0, 3), (0, 4), (0, 5)],
+    "second_back": [("F", 6), (2, 1)],
+    "context_back": [(1, 3), (0, 6)],
     "backward": {
-        0: [(2, 2), (1, 4)],
-        1: [(3, 1), (1, 5), (1, 6), (0, 7)],
-        2: [(4, 0), (3, 2), (2, 3), (1, 7)],
-        3: [(4, 1), (0, 8)],
-        4: [(5, 1), (4, 2), (2, 4), (1, 8)],
+        0: [(3, 0), (2, 2), (1, 4)],
+        1: [(1, 5), (1, 6), (0, 7), (3, 1)],
+        2: [(3, 2), (2, 3), (1, 7)],
+        3: [(4, 0), (0, 8)],
+        4: [(4, 2), (2, 4), (1, 8)],
         5: [(3, 3), (2, 5), (0, 9)],
-        6: [(2, 7), (1, 9)],
-        7: [(5, 0), (5, 2), (3, 4), (2, 6), (2, 8), (0, 10)],
-        8: [(6, 0), (6, 2), (4, 3), (3, 5), (1, 10)],
-        9: [(5, 3), (4, 4), (3, 6), (3, 7), (2, 9), (0, 11)],
-        10: [(6, 3), (5, 4), (4, 7), (3, 8), (2, 10), (1, 11)],
-        11: [(4, 5), (4, 6), (5, 7), (4, 8), (0, 12)],
+        6: [(2, 6), (2, 7), (1, 9)],
+        7: [(5, 0), (4, 1), (5, 2), (3, 4), (2, 8), (0, 10)],
+        8: [(6, 0), (5, 1), (6, 2), (4, 3), (3, 5), (1, 10)],
+        9: [(5, 3), (4, 4), (3, 6), (3, 7), (0, 11)],
+        10: [(6, 3), (5, 4), (4, 7), (3, 8), (2, 9), (1, 11)],
+        11: [(4, 5), (5, 7), (4, 8), (2, 10), (0, 12)],
     },
     "attention_back": [],
     "last": {
-        1: [(5, 8), (2, 11)],
-        2: [(5, 5), (5, 6), (3, 9), (1, 12)],
-        3: [(6, 5), (3, 10), (6, 6)],
+        0: [(1, 12), (4, 6), (5, 8), (2, 11)],
+        1: [(5, 5), (3, 9)],
+        2: [(2, 12), (6, 5), (5, 6)],
+        3: [(4, 9), (3, 10)],
     },
-    "tail_one": [(4, 9), (3, 11)],
-    "tail_two": [(5, 9), (4, 10), (2, 12)],
-    "tail_three": [(4, 11), (5, 10), (5, 11), (3, 12), (4, 12), (5, 12)],
+    "tail_one": [(6, 6), (5, 9), (3, 11)],
+    "tail_two": [(4, 10), (3, 12)],
+    "tail_three": [(4, 11), (5, 10), (4, 12), (5, 11), (5, 12)],
 }
 
 
@@ -366,14 +390,22 @@
 
 
 class Gather:
-    def __init__(self, place, ref, rows, half, skip, along_sems, hop_sems):
+    def __init__(self, place, ref, rows, base, half, skip, by_rows, along_sems, hop_sems):
         self.p, self.ref, self.half, self.skip = place, ref, half, skip
-        self.rows, self.along_sems, self.hop_sems = pl.ds(*rows), along_sems, hop_sems
+        self.along_sems, self.hop_sems = along_sems, hop_sems
+        first, held = rows
+        if by_rows:
+            self.rows = pl.ds(aligned(first + place.core * held, 16), held)
+            self.base = base
+        else:
+            self.rows = pl.ds(first, held)
+            self.base = base + place.core * half
 
     def carried(self):
         p = self.p
         return pl.ds(
-            aligned(p.core * self.half + p.x * self.skip, 128), self.half - self.skip
+            aligned(self.base + p.x * self.skip, 128),
+            self.half - self.skip,
         )
 
     def own(self):
@@ -404,13 +436,13 @@
 
     def copy_x(self):
         p = self.p
-        start = p.core * self.half + p.x * (self.half - self.skip)
+        start = self.base + p.x * (self.half - self.skip)
         part = self.ref.at[:, :, self.rows, pl.ds(aligned(start, 128), self.skip)]
         return self.hop(1, part, p.across())
 
     def copy_core(self):
         p = self.p
-        part = self.ref.at[:, :, self.rows, pl.ds(aligned(p.core * self.half, 128), self.half)]
+        part = self.ref.at[:, :, self.rows, pl.ds(aligned(self.base, 128), self.half)]
         return self.hop(2, part, p.sibling())
 
     def start_z(self):
@@ -424,10 +456,12 @@
 
     def start_x(self):
         self.copy_y().wait_recv()
-        self.copy_x().start()
+        if self.skip:
+            self.copy_x().start()
 
     def start_core(self):
-        self.copy_x().wait_recv()
+        if self.skip:
+            self.copy_x().wait_recv()
         self.copy_core().start()
 
     def arrive(self):
@@ -437,7 +471,8 @@
         for copy in self.copies_z():
             copy.wait_send()
         self.copy_y().wait_send()
-        self.copy_x().wait_send()
+        if self.skip:
+            self.copy_x().wait_send()
         self.copy_core().wait_send()
 
 
@@ -568,11 +603,11 @@
 def layer(config, *refs):
     (reps, group, count, width, heads, hidden, tasks_held) = config
     (
-        lengths_ref, tasks_ref, small_ref, patches_ref, cot_ref,
+        lengths_ref, tasks_ref, gain_one_ref, gain_two_ref, table_ref, patches_ref, cot_ref,
         wq_ref, wk_ref, wv_ref, wo_ref, wg_ref, wu_ref, wd_ref,
         out_ref, grad_ref, done_in, done_gate, done_up, done_down, done_small, spare,
         w_in, w_out, w_ff, w_down,
-        normed, qkv, context, extra, mixed, tokens, second, hid, gate_g, up_g,
+        normed, qkv, context, extra, mixed, tokens, second, hid, both_g,
         acc_out, acc_in, key_extra, vectors, small_buf, small_grads, member_buf, peer_out, peer_buf,
         *rest,
     ) = refs
@@ -592,73 +627,78 @@
     specs = []
     cuts = [0]
 
-    def spec(ref, half, skip, parts):
+    def spec(ref, base, half, skip):
+        parts = PARTS[len(cuts) - 1]
         held_rows = ref.shape[2] // parts
         for i in range(parts):
-            specs.append((ref, (i * held_rows, held_rows), half, skip))
+            specs.append((ref, (i * held_rows, held_rows), base, half, skip, False))
         cuts.append(len(specs))
 
-    for g in range(groups):
-        spec(w_in.at[g], 384, 128, PARTS[g])
-    spec(w_out.at[0], 384, 128, PARTS[groups])
+    pairs = 2 * groups
+    for pair in range(pairs):
+        specs.append((w_in.at[pair // 2], (0, rows // 2), (pair % 2) * 384, 384, 128, True))
+        cuts.append(len(specs))
+    spec(w_out.at[0], 0, 384, 128)
     for j in range(2):
-        spec(w_ff.at[j], 512, 128, PARTS[groups + 1 + 3 * j])
-        spec(w_ff.at[2 + j], 512, 256 - 128 * j, PARTS[groups + 2 + 3 * j])
-        spec(w_down.at[j], 384, 128, PARTS[groups + 3 + 3 * j])
-    chunks = [
-        Gather(p, ref, held_rows, half, skip, along_sems.at[i], hop_sems.at[i])
-        for i, (ref, held_rows, half, skip) in enumerate(specs)
-    ]
+        for u in range(2):
+            spec(w_ff.at[j], u * 512, 256, 128)
+            spec(w_ff.at[2 + j], u * 512, 256, UP_SKIP[2 * j + u])
+            if u == 0:
+                spec(w_down.at[j], 0, 384, 128)
+    chunks = [Gather(p, *one, along_sems.at[i], hop_sems.at[i]) for i, one in enumerate(specs)]
 
     sem = 0
     fills = [[] for _ in PARTS]
-    for g in range(groups):
+    own_rows = pl.ds(aligned(p.core * (rows // 2), 16), rows // 2)
+    for pair in range(pairs):
         for i in range(2):
-            start = pl.ds(aligned(g * 256 + p.core * 128, 128), 128)
-            target = w_in.at[g, p.z, p.y, :, pl.ds(aligned(p.core * 384 + (p.x + i) * 128, 128), 128)]
-            pair = (wq_ref, wk_ref) if i == 0 else (wk_ref, wv_ref)
-            fills[g].append(
+            source = pl.ds(pair * 128, 128)
+            start = (pair % 2) * 384 + (p.x + i) * 128
+            target = w_in.at[pair // 2, p.z, p.y, own_rows, pl.ds(aligned(start, 128), 128)]
+            choice = (wq_ref, wk_ref) if i == 0 else (wk_ref, wv_ref)
+            fills[pair].append(
                 tuple(
-                    pltpu.make_async_copy(w.at[:, start], target, local_sems.at[sem]) for w in pair
+                    pltpu.make_async_copy(w.at[own_rows, source], target, local_sems.at[sem])
+                    for w in choice
                 )
             )
             sem += 1
     columns = pl.ds(aligned(p.core * 384 + p.x * 128, 128), 256)
-    fills[groups].append(
+    fills[pairs].append(
         pltpu.make_async_copy(
             wo_ref.at[:, columns], w_out.at[0, p.z, p.y, :, columns], local_sems.at[sem]
         )
     )
     sem += 1
+    at = pairs + 1
+
+    def fill(source, target):
+        nonlocal sem
+        fills[at].append(pltpu.make_async_copy(source, target, local_sems.at[sem]))
+        sem += 1
+
+    def segment(ref, held, j, seg):
+        fill(
+            ref.at[:, pl.ds(aligned(seg * 256 + j * 128, 128), 128)],
+            held.at[p.z, p.y, :, pl.ds(aligned(seg * 128, 128), 128)],
+        )
+
     for j in range(2):
-        for i in range(3):
-            seg = 4 * p.core + p.x + i
-            fills[groups + 1 + 3 * j].append(
-                pltpu.make_async_copy(
-                    wg_ref.at[:, pl.ds(aligned(seg * 256 + j * 128, 128), 128)],
-                    w_ff.at[j, p.z, p.y, :, pl.ds(aligned(seg * 128, 128), 128)],
-                    local_sems.at[sem],
+        for u in range(2):
+            segment(wg_ref, w_ff.at[j], j, 4 * u + 2 * p.core + p.x)
+            at += 1
+            if UP_SKIP[2 * j + u]:
+                segment(wu_ref, w_ff.at[2 + j], j, 4 * u + 2 * p.core + p.x)
+            else:
+                for i in range(2):
+                    segment(wu_ref, w_ff.at[2 + j], j, 4 * u + 2 * p.core + i)
+            at += 1
+            if u == 0:
+                fill(
+                    wd_ref.at[pl.ds(j * down_rows, down_rows), columns],
+                    w_down.at[j, p.z, p.y, :, columns],
                 )
-            )
-            sem += 1
-        for i in range(2 + j):
-            seg = 4 * p.core + (2 - j) * p.x + i
-            fills[groups + 2 + 3 * j].append(
-                pltpu.make_async_copy(
-                    wu_ref.at[:, pl.ds(aligned(seg * 256 + j * 128, 128), 128)],
-                    w_ff.at[2 + j, p.z, p.y, :, pl.ds(aligned(seg * 128, 128), 128)],
-                    local_sems.at[sem],
-                )
-            )
-            sem += 1
-        fills[groups + 3 + 3 * j].append(
-            pltpu.make_async_copy(
-                wd_ref.at[pl.ds(j * down_rows, down_rows), columns],
-                w_down.at[j, p.z, p.y, :, columns],
-                local_sems.at[sem],
-            )
-        )
-        sem += 1
+                at += 1
 
     def fill_start(i):
         for copy in fills[i]:
@@ -684,7 +724,7 @@
             (w_down.at[j], done_down.at[j], True),
         ]
     grads += [(w_out.at[0], done_in.at[groups], True)]
-    for pair in range(2 * groups):
+    for pair in range(pairs):
         columns = pl.ds((pair % 2) * 384, 384)
         grads.append(
             (
@@ -701,7 +741,15 @@
     tokens_in.start()
     for i in range(len(fills)):
         fill_start(i)
-    small_buf[p.pos] = small_ref[...]
+    shard = width // group
+    own_small = jnp.concatenate(
+        [ref[...].astype(F32) for ref in (gain_one_ref, gain_two_ref, table_ref)]
+        + [jnp.zeros((14 - tasks_held, shard), F32)],
+        0,
+    )
+    small_buf[p.pos] = jnp.concatenate(
+        [own_small, jnp.zeros((16, 128 - shard), F32)], 1
+    ).astype(BF16)
     barrier = pltpu.get_barrier_semaphore()
     for step in range(1, reps):
         pl.semaphore_signal(barrier, inc=1, device_id=p.member(step), device_id_type=MESH)
@@ -741,7 +789,6 @@
 
     for copy in small_copies:
         copy.wait_recv()
-    shard = width // group
     wide_row = lax.broadcasted_iota(jnp.int32, (128, width), 0)
     wide_col = lax.broadcasted_iota(jnp.int32, (128, width), 1)
     total = None
@@ -780,21 +827,21 @@
         normed[r, :] = (resid * inv * vectors[0:1, :]).astype(BF16)
         return 0
 
+    go(*EVENTS["ready"])
     lax.fori_loop(0, blocks, norm_one, 0)
 
     go(*EVENTS["pre"])
 
-    def project(g):
-        for core in range(2):
-            base = core * 384
-            weight = w_in[g, :, :, :, base : base + 384].reshape(width, 384)
-            got = dot(weight, normed[...], 0, 1)
-            qkv[g, base : base + 128] = (got[:128] * scale).astype(BF16)
-            qkv[g, base + 128 : base + 384] = got[128:].astype(BF16)
+    def project(pair):
+        g = pair // 2
+        base = aligned((pair % 2) * 384, 128)
+        weight = w_in[g, :, :, :, pl.ds(base, 384)].reshape(width, 384)
+        got = dot(weight, normed[...], 0, 1)
+        qkv[g, pl.ds(base, 128)] = (got[:128] * scale).astype(BF16)
+        qkv[g, pl.ds(base + 128, 256)] = got[128:].astype(BF16)
 
     tile = 256
     tiles = count // tile
-    wide = count // 2
     sixteen = lax.broadcasted_iota(jnp.int32, (16, count), 0)
 
     def offsets(h):
@@ -839,9 +886,8 @@
         missing = (exact - low.astype(F32)).astype(BF16)
         r = pl.ds(aligned(h * head_dim, 64), head_dim)
         context[r, :] = low
-        hid[r, :] = missing[:, :wide]
-        gate_g[r, :] = missing[:, wide:]
-        extra[h, 0:16] = splits(-(top + jnp.log(total)), 1.0)
+        both_g[r, :] = missing
+        extra[0, pl.ds(h, 1), :] = -(top + jnp.log(total))
 
     def splits(row, fourth):
         high = row.astype(BF16).astype(F32)
@@ -864,25 +910,25 @@
             def _(events=events):
                 go(*events)
 
-        @pl.when(h % quad == 0)
+        @pl.when(h % 2 == 0)
         def _():
-            project(h // quad)
+            project(h // 2)
+
+        for at, events in EVENTS["projected"].items():
+
+            @pl.when(h == at)
+            def _(events=events):
+                go(*events)
 
         forward_head(h)
         return 0
 
     lax.fori_loop(0, heads, each_head, 0)
-    kept = [hid.at[pl.ds(0, width), :], gate_g.at[pl.ds(0, width), :]]
+    kept = both_g.at[pl.ds(0, width), :]
     first_out = 6 + len(grads)
-    keep = [
-        pltpu.make_async_copy(kept[i], spare.at[i], out_sems.at[first_out + i]) for i in range(2)
-    ]
-    fetch = [
-        pltpu.make_async_copy(spare.at[i], kept[i], out_sems.at[first_out + 2 + i])
-        for i in range(2)
-    ]
-    for copy in keep:
-        copy.start()
+    keep = pltpu.make_async_copy(kept, spare, out_sems.at[first_out])
+    fetch = pltpu.make_async_copy(spare, kept, out_sems.at[first_out + 1])
+    keep.start()
     go(*EVENTS["attended"])
 
     big = 256
@@ -892,6 +938,8 @@
         m = tokens[r, :].astype(F32) + task_row()
         m = m + dot(context[:, r], w_out[0].reshape(width, width), 0, 0)
         mixed[r, :] = m
+        acc_out[r, :] = m
+        acc_in[r, :] = jnp.zeros_like(m)
         inv = lax.rsqrt(jnp.mean(m * m, axis=-1, keepdims=True) + EPS)
         second[r, :] = (m * inv * vectors[1:2, :]).astype(BF16)
         return 0
@@ -905,8 +953,7 @@
     curve = 0.7978845608028654
     cube = 0.044715
     part = 512
-    for copy in keep:
-        copy.wait()
+    keep.wait()
 
     def ff_tile(t, _):
         j, u = t // 2, t % 2
@@ -939,28 +986,19 @@
             g_grad = (back * up * slope).astype(BF16)
             u_grad = (back * gelu).astype(BF16)
             hid[r, :] = h
-            gate_g[r, :] = g_grad
-            up_g[r, :] = u_grad
+            both_g[r, 0:part] = g_grad
+            both_g[r, part : 2 * part] = u_grad
             o = dot(h, down_w, 1, 0)
             n = dot(g_grad, gate_w, 1, 1) + dot(u_grad, up_w, 1, 1)
-
-            @pl.when(t == 0)
-            def _():
-                acc_out[r, :] = o
-                acc_in[r, :] = n
-
-            @pl.when(t > 0)
-            def _():
-                acc_out[r, :] = acc_out[r, :] + o
-                acc_in[r, :] = acc_in[r, :] + n
-
+            acc_out[r, :] = acc_out[r, :] + o
+            acc_in[r, :] = acc_in[r, :] + n
             return 0
 
         lax.fori_loop(0, count // big, block_of, 0)
         def pause(k):
             for at, events in EVENTS["outer"].items():
 
-                @pl.when(t * 3 + k == at)
+                @pl.when(t * 2 + k == at)
                 def _(events=events):
                     go(*events)
 
@@ -969,18 +1007,17 @@
             dot(hid[...], tokens[...], 0, 0).astype(BF16).reshape(deep // 2, 2, down_rows, width)
         )
         pause(1)
-        w_ff[j, :, :, :, cols] = (
-            dot(second[...], gate_g[...], 0, 0).astype(BF16).reshape(deep, 2, rows, part)
-        )
-        pause(2)
-        w_ff[2 + j, :, :, :, cols] = (
-            dot(second[...], up_g[...], 0, 0).astype(BF16).reshape(deep, 2, rows, part)
-        )
+        for v in range(2):
+            some = slice(v * width // 2, (v + 1) * width // 2)
+            to = slice(v * deep // 2, (v + 1) * deep // 2)
+            both = dot(second[:, some], both_g[...], 0, 0).astype(BF16)
+            both = both.reshape(deep // 2, 2, rows, 2 * part)
+            w_ff[j, to, :, :, cols] = both[..., :part]
+            w_ff[2 + j, to, :, :, cols] = both[..., part:]
         return 0
 
     lax.fori_loop(0, 4, ff_tile, 0)
-    for copy in fetch:
-        copy.start()
+    fetch.start()
     go(*EVENTS["ff_done"])
 
     small_grads[...] = jnp.zeros_like(small_grads)
@@ -988,7 +1025,7 @@
     def second_back(i, _):
         r = rows_of(i)
         m = mixed[r, :]
-        second[r, :] = (m + acc_out[r, :]).astype(BF16)
+        second[r, :] = acc_out[r, :].astype(BF16)
         inv = lax.rsqrt(jnp.mean(m * m, axis=-1, keepdims=True) + EPS)
         unit = m * inv
         got = acc_in[r, :]
@@ -1009,16 +1046,13 @@
     out_w = w_out[0].reshape(width, width)
     acc_out[0:width, :] = dot(context[...], tokens[...], 1, 0)
     lowered = dot(out_w, tokens[...], 1, 1).astype(BF16)
-    for copy in fetch:
-        copy.wait()
+    fetch.wait()
     for h in range(heads):
         r = slice(h * head_dim, (h + 1) * head_dim)
         low = lowered[r]
-        exact = context[r, :].astype(F32) + jnp.concatenate(
-            [hid[r, :], gate_g[r, :]], 1
-        ).astype(F32)
+        exact = context[r, :].astype(F32) + both_g[r, :].astype(F32)
         delta = jnp.sum(low.astype(F32) * exact, axis=0, keepdims=True)
-        extra[h, 16:32] = splits(-delta, 0.0)
+        extra[1, h : h + 1, :] = -delta
         context[r, :] = low
     w_out[0] = acc_out[0:width, :].astype(BF16).reshape(deep, 2, rows, width)
     go(*EVENTS["context_back"])
@@ -1029,16 +1063,18 @@
         k_rows = pl.ds(aligned(off + 128, 64), head_dim)
         v_rows = pl.ds(aligned(off + 256, 64), head_dim)
         query = qkv[g, q_rows, :]
+        all_keys = qkv[g, k_rows, :]
+        all_vals = qkv[g, v_rows, :]
         back = context[pl.ds(aligned(h * head_dim, 64), head_dim), :]
-        ask = jnp.concatenate([query, extra[h, 0:16]], 0)
-        back_ask = jnp.concatenate([back, extra[h, 16:32]], 0)
+        ask = jnp.concatenate([query, splits(extra[0, pl.ds(h, 1), :], 1.0)], 0)
+        back_ask = jnp.concatenate([back, splits(extra[1, pl.ds(h, 1), :], 0.0)], 0)
         query_grad = None
         for j in range(tiles):
             cut = slice(j * tile, (j + 1) * tile)
-            keys = qkv[g, k_rows, cut]
+            keys = all_keys[:, cut]
             lift = key_extra[:, cut]
             probs = jnp.exp(dot(jnp.concatenate([keys, lift], 0), ask, 0, 0))
-            gap = dot(jnp.concatenate([qkv[g, v_rows, cut], lift], 0), back_ask, 0, 0)
+            gap = dot(jnp.concatenate([all_vals[:, cut], lift], 0), back_ask, 0, 0)
             score_grad = (probs * gap).astype(BF16)
             part = dot(keys, score_grad, 1, 0)
             query_grad = part if query_grad is None else query_grad + part
@@ -1173,47 +1209,69 @@
 
 def ending(config, *refs):
     groups, group, rows, held = config
-    output, grad, done_in, done_gate, done_up, done_down, done_small = refs[:7]
-    out, out_grad, query, key, value, proj, gate, up, down, one, two, table = refs[7:19]
-    sems = refs[19]
-    held_out, held_grad = refs[20:22]
+    sources, small = refs[:6], refs[6]
+    targets, (one, two, table) = refs[7:16], refs[16:19]
+    in_sems, out_sems = refs[19:21]
+    held_out, held_grad, from_in, from_gate, from_up, from_down = refs[21:27]
+    made = refs[27:34]
     parts = 4
-    span = output.shape[0] // parts
+    span = held_out.shape[0] // parts
     brought, copies = [], []
+    middles = (from_in, from_gate, from_up, from_down)
+    for i, (source, middle) in enumerate(zip(sources[2:], middles)):
+        brought.append(pltpu.make_async_copy(source, middle, in_sems.at[i]))
+        brought[-1].start()
+    whole = []
     for i in range(parts):
         r = pl.ds(i * span, span)
-        for k, (source, middle, target) in enumerate(
-            ((output, held_out, out.at[0]), (grad, held_grad, out_grad.at[0]))
-        ):
-            brought.append(
-                pltpu.make_async_copy(source.at[r], middle.at[r], sems.at[0, k, i])
+        for k, middle in enumerate((held_out, held_grad)):
+            at = 4 + 2 * i + k
+            whole.append(
+                (
+                    pltpu.make_async_copy(sources[k].at[r], middle.at[r], in_sems.at[at]),
+                    pltpu.make_async_copy(middle.at[r], targets[k].at[0, r], out_sems.at[at]),
+                )
             )
-            copies.append(
-                pltpu.make_async_copy(middle.at[r], target.at[r], sems.at[1, k, i])
-            )
-    for copy in brought:
-        copy.start()
-    for first, then in zip(brought, copies):
-        first.wait()
-        then.start()
-    for g in range(groups):
-        for core in range(2):
-            for i, ref in enumerate((query, key, value)):
+            whole[-1][0].start()
+
+    def finish(i):
+        copies.append(pltpu.make_async_copy(made[i], targets[2 + i], out_sems.at[12 + i]))
+        copies[-1].start()
+
+    def pass_on(count):
+        for _ in range(count):
+            first, then = whole.pop(0)
+            first.wait()
+            then.start()
+            copies.append(then)
+
+    brought[0].wait()
+    for i in range(3):
+        for g in range(groups):
+            for core in range(2):
                 start = core * 384 + i * 128
                 to = g * 256 + core * 128
-                ref[:, to : to + 128] = done_in[g, :, start : start + 128].astype(F32)
-    proj[...] = done_in[groups].astype(F32)
-    for done, ref in ((done_gate, gate), (done_up, up)):
+                made[i][:, to : to + 128] = from_in[g, :, start : start + 128].astype(F32)
+        finish(i)
+    made[3][...] = from_in[groups].astype(F32)
+    finish(3)
+    for k, source in enumerate((from_gate, from_up)):
+        brought[1 + k].wait()
         for j in range(2):
             for f in range(group):
                 to = f * 256 + j * 128
-                ref[:, to : to + 128] = done[j, :, f * 128 : (f + 1) * 128].astype(F32)
-    half = done_down.shape[1]
+                made[4 + k][:, to : to + 128] = source[j, :, f * 128 : (f + 1) * 128].astype(F32)
+        finish(4 + k)
+        pass_on(2)
+    brought[3].wait()
+    half = from_down.shape[1]
     for j in range(2):
-        down[j * half : (j + 1) * half, :] = done_down[j].astype(F32)
-    one[...] = done_small[0, :rows]
-    two[...] = done_small[1, :rows]
-    table[...] = done_small[...].T[:rows, 2 : 2 + held]
+        made[6][j * half : (j + 1) * half, :] = from_down[j].astype(F32)
+    finish(6)
+    pass_on(4)
+    one[...] = small[0, :rows]
+    two[...] = small[1, :rows]
+    table[...] = small[2 : 2 + held, :rows]
     for copy in copies:
         copy.wait()
 
@@ -1228,8 +1286,6 @@
     deep = group // PAIR
     groups = width // 256
     down_rows = w_down.shape[0] // 2
-    small = jnp.concatenate([gain_attn[None], gain_mlp[None], task_table.T], axis=0)
-    small = jnp.pad(small, ((0, 16 - small.shape[0]), (0, 128 - rows)))
 
     def of(rows, columns, x_first, by_rows=False):
         whole = (rows, columns)
@@ -1272,13 +1328,12 @@
         pltpu.VMEM((count, width), BF16),
         pltpu.VMEM((groups, width, count), BF16),
         pltpu.VMEM((width, count), BF16),
-        pltpu.VMEM((HEADS, 32, count), BF16),
+        pltpu.VMEM((2, 16, count), F32),
         pltpu.VMEM((count, width), F32),
         pltpu.VMEM((count, width), BF16),
         pltpu.VMEM((count, width), BF16),
         pltpu.VMEM((count, 512), BF16),
-        pltpu.VMEM((count, 512), BF16),
-        pltpu.VMEM((count, 512), BF16),
+        pltpu.VMEM((count, 1024), BF16),
         pltpu.VMEM((count, width), F32),
         pltpu.VMEM((count, width), F32),
         pltpu.VMEM((16, count), BF16),
@@ -1288,7 +1343,7 @@
         pltpu.VMEM((reps, 8, width), F32),
         pltpu.VMEM((group, 8, 128), F32),
         pltpu.VMEM((group, 8, 128), F32),
-        pltpu.SemaphoreType.DMA((groups * 2 + 1 + 13,)),
+        pltpu.SemaphoreType.DMA((groups * 4 + 1 + 14,)),
         pltpu.SemaphoreType.DMA((chunks, 2, deep - 1)),
         pltpu.SemaphoreType.DMA((chunks, 2, 3)),
         pltpu.SemaphoreType.DMA((2, group - 1)),
@@ -1312,9 +1367,9 @@
             shape((2, rows, hidden // 2), BF16),
             shape((2, down_rows, width), BF16),
             shape((8, 128), F32),
-            shape((2, width, count // 2), BF16),
+            shape((width, count), BF16),
         ],
-        in_specs=[smem, smem, pl.BlockSpec(memory_space=pltpu.VMEM)] + [anywhere] * 9,
+        in_specs=[smem, smem] + [pl.BlockSpec(memory_space=pltpu.VMEM)] * 3 + [anywhere] * 9,
         out_specs=[anywhere] * 8,
         scratch_shapes=scratch,
         compiler_params=pltpu.CompilerParams(
@@ -1322,32 +1377,38 @@
         ),
         name="layer",
     )(
-        lengths, tasks, small, patches[0], cotangent[0],
+        lengths, tasks, gain_attn[None], gain_mlp[None], task_table.T, patches[0], cotangent[0],
         w_query, w_key, w_value, w_out, w_gate, w_up, w_down,
     )
     lane = pl.BlockSpec(memory_space=pltpu.VMEM)
-    return pl.pallas_call(
+    sizes = [(rows, width)] * 4 + [(rows, hidden)] * 2 + [(2 * down_rows, width)]
+    results = pl.pallas_call(
         functools.partial(ending, (groups, group, rows, held)),
         out_shape=[
             shape((1, count, width), BF16),
             shape((1, count, width), F32),
-            *[shape((rows, width), F32)] * 4,
-            *[shape((rows, hidden), F32)] * 2,
-            shape((2 * down_rows, width), F32),
+            *[shape(size, F32) for size in sizes],
             shape((rows,), F32),
             shape((rows,), F32),
-            shape((rows, held), F32),
+            shape((held, rows), F32),
         ],
-        in_specs=[anywhere] * 2 + [lane] * 5,
-        out_specs=[anywhere] * 2 + [lane] * 10,
+        in_specs=[anywhere] * 6 + [lane],
+        out_specs=[anywhere] * 9 + [lane] * 3,
         scratch_shapes=[
-            pltpu.SemaphoreType.DMA((2, 2, 4)),
+            pltpu.SemaphoreType.DMA((12,)),
+            pltpu.SemaphoreType.DMA((19,)),
             pltpu.VMEM((count, width), BF16),
             pltpu.VMEM((count, width), F32),
+            pltpu.VMEM((groups + 1, rows, width), BF16),
+            pltpu.VMEM((2, rows, hidden // 2), BF16),
+            pltpu.VMEM((2, rows, hidden // 2), BF16),
+            pltpu.VMEM((2, down_rows, width), BF16),
+            *[pltpu.VMEM(size, F32) for size in sizes],
         ],
         compiler_params=pltpu.CompilerParams(vmem_limit_bytes=62 * 1024 * 1024),
         name="ending",
     )(output, grad, done_in, done_gate, done_up, done_down, done_small)
+    return (*results[:11], results[11].T)
 
 
 def solution(mesh):

time: 205 us -> 197 us (0.961)
  Pallas kernels: 200 us -> 195 us
    pallas_call x1, Pallas kernels: 193 us -> 188 us  [fused(): pl.pallas_call(functools.partial(layer, config), out_shape=[shape((count,...]
where the time goes in v3:
time: 197 us
  Pallas kernels  195 us (99%)
  between operations  2.11 us (1%)
    pallas_call x1, Pallas kernels, fused(): pl.pallas_call(functools.partial(layer, config), out_shape=[shape((count,...  188 us
    pallas_call x1, Pallas kernels, fused(): pl.pallas_call(functools.partial(ending, (groups, group, rows, held)), ou...  7.32 us

profile of v3, /device:TPU:0, one launch (start us, length us, event | category | flops | bytes accessed | tf_op | source)
XLA Modules:
  0.0 197.2 jit_solution(14176923848091752553)
XLA Ops:
  1.9 187.8 %layer.1 = (bf16[1024,768]{1,0:T(8,128)(2,1)}, f32[1024,768]{1,0:T(8,128)}, bf16[4,96,768]{2,1,0:T(8,128)(2,1)}, bf16[2,96,1024]{2,1,0:T(8,128)(2,1)}, bf16[2,96...) custom-call(s32[1]{0:T(128)S(6)} %copy.26.refs_0_, ...), custom_call_target="tpu_custom_call" | custom-call | tf_op jit(solution)/shard_map/layer/pallas_call | solution.py:1360
  189.8 7.3 %ending.1 = (bf16[1,1024,768]{2,1,0:T(8,128)(2,1)}, f32[1,1024,768]{2,1,0:T(8,128)}, f32[96,768]{1,0:T(8,128)}, f32[96,768]{1,0:T(8,128)}, f32[96,768]{1,0:T(8,1...) custom-call(bf16[1024,768]{1,0:T(8,128)(2,1)} %get-tuple-element.31., ...), custom_call_target="tpu_custom_call" | custom-call | tf_op jit(solution)/shard_map/ending/pallas_call | solution.py:1385

commit v4 on v3

--- a/solution.py
+++ b/solution.py
@@ -231,104 +231,93 @@
     )
 
 
-PARTS = [1, 1, 1, 1, 1, 1, 1, 2, 2, 2, 2, 2, 2, 2, 2, 2, 2]
-
-UP_SKIP = (0, 128, 0, 128)
+PARTS = [1, 1, 1, 1, 1, 1, 1, 2, 1, 2, 1, 1, 1, 1, 2, 1, 1]
+
+UP_SKIP = (0, 0, 0, 128)
+
+LAST_PARTS = 3
 
 EVENTS = {
-    "start": [("Z", 0), ("Z", 1), ("Z", 2)],
-    "ready": [],
+    "start": [("Z", 0), ("Z", 1)],
+    "ready": [("Z", 2)],
     "pre": [
-        ("Y", 0), ("Z", 3), ("Z", 4), ("Y", 1), ("X", 0), ("Z", 5), ("Y", 2), ("X", 1), ("Z", 6),
-        ("Y", 3), ("C", 0), ("X", 2), ("Y", 4), ("D", 0), ("Z", 7),
+        ("Y", 0), ("Z", 3), ("Y", 1), ("X", 0), ("Z", 4), ("Y", 2), ("X", 1), ("Z", 5), ("Y", 3),
+        ("C", 0), ("Z", 6), ("X", 2), ("Y", 4), ("D", 0),
     ],
     "forward": {
-        1: [("X", 3), ("Y", 5), ("Z", 9)],
-        2: [("D", 1), ("C", 2), ("X", 4), ("Z", 10)],
-        3: [("C", 3), ("X", 5), ("Y", 6), ("Z", 11)],
-        4: [("D", 2), ("Y", 7), ("Y", 8)],
-        5: [("C", 5), ("Y", 9)],
-        6: [("D", 3), ("Z", 13)],
-        7: [("X", 7), ("X", 8), ("Z", 15), ("Z", 16)],
-        8: [("D", 4), ("Y", 11), ("Z", 17)],
-        9: [("C", 9), ("Y", 12), ("Y", 13), ("Z", 19), ("X", 10)],
-        10: [("D", 5), ("C", 6), ("C", 10), ("Y", 14), ("Z", 20)],
-        11: [("Y", 16), ("Y", 17), ("Z", 21)],
+        1: [("X", 3), ("Y", 5), ("Z", 7)],
+        2: [("D", 1), ("C", 2), ("X", 4), ("Z", 8), ("Z", 9)],
+        3: [("C", 3), ("X", 5), ("Y", 6)],
+        4: [("D", 2), ("C", 4), ("Y", 7), ("Y", 8), ("Z", 10)],
+        5: [("C", 5), ("Z", 11)],
+        6: [("D", 3), ("X", 6), ("Y", 9)],
+        7: [("X", 8), ("Y", 10), ("Z", 13)],
+        8: [("D", 4)],
+        9: [("C", 6), ("X", 9), ("Y", 12), ("Z", 14)],
+        10: [("D", 5), ("C", 7), ("C", 9), ("X", 10), ("Z", 15)],
+        11: [("X", 11), ("Y", 13)],
     },
     "projected": {
-        0: [("C", 1), ("Z", 8)],
-        4: [("C", 4), ("Z", 12)],
-        6: [("X", 6), ("Y", 10), ("Z", 14)],
-        8: [("X", 9), ("Z", 18)],
-        10: [("C", 7), ("Y", 15), ("X", 11)],
+        0: [("C", 1)],
+        6: [("X", 7), ("Z", 12)],
+        8: [("Y", 11)],
+        10: [("C", 8)],
     },
     "attended": [
-        ("D", 6), ("C", 8), ("X", 12), ("Y", 18), ("Z", 22), ("F", 0), ("F", 1), ("F", 2),
+        ("D", 6), ("C", 10), ("X", 12), ("Y", 14), ("Z", 16), ("F", 0), ("F", 1), ("F", 2),
         ("F", 3), ("F", 4), ("F", 5),
     ],
-    "normed": [("C", 11), ("X", 13), ("X", 14), ("X", 15), ("Y", 19), ("Z", 23)],
+    "project": {
+    },
+    "normed": [("C", 11), ("Z", 17)],
     "block": {
-        0: [
-            ("D", 7), ("D", 8), ("D", 9), ("D", 10), ("Y", 20), ("X", 16), ("C", 12), ("Z", 24),
-            ("X", 17), ("D", 11), ("Z", 25), ("X", 18), ("Y", 21), ("C", 13), ("Z", 26), ("D", 12),
-        ],
-        2: [("C", 14), ("X", 19)],
-        3: [("C", 19), ("X", 20), ("Y", 22), ("Y", 23)],
-        4: [
-            ("D", 13), ("D", 14), ("D", 15), ("C", 16), ("Y", 26), ("C", 17), ("X", 22), ("X", 23),
-            ("C", 18), ("D", 16),
-        ],
-        5: [("X", 24)],
-        6: [("X", 25)],
-        7: [("C", 21), ("X", 26)],
-        8: [
-            ("D", 17), ("D", 18), ("D", 19), ("D", 20), ("D", 21), ("C", 23), ("D", 22), (0, 0),
-            (0, 1), (0, 2),
-        ],
-        9: [("C", 24)],
-        11: [("C", 25)],
-        12: [("D", 23), ("D", 24), ("D", 25), ("D", 26), (1, 1), (1, 2)],
+        0: [("D", 7), ("D", 8), ("D", 9), ("D", 10), ("Y", 15), ("X", 13), ("C", 13), ("D", 11)],
+        1: [("X", 14), ("Z", 18)],
+        2: [("C", 12), ("Y", 16), ("Z", 19)],
+        4: [("D", 12), ("D", 13), ("X", 16), ("Y", 19)],
+        5: [("X", 17)],
+        7: [("C", 16), ("X", 18)],
+        8: [("D", 14), ("D", 15), ("D", 16), ("D", 17), (0, 0), (0, 1), (0, 2)],
+        10: [("C", 18)],
+        12: [("D", 18), ("D", 19), (1, 2)],
     },
     "outer": {
-        0: [
-            ("F", 7), ("F", 8), ("F", 9), ("F", 10), ("F", 11), ("F", 12), ("C", 15), ("C", 20),
-            ("Y", 24),
-        ],
-        1: [("X", 21), ("Y", 25)],
-        2: [("F", 13), ("F", 14), ("F", 15), ("F", 16)],
-        3: [("C", 22)],
-        4: [("F", 17), ("F", 18), ("F", 19), ("F", 20), ("F", 21), ("F", 22), (1, 0)],
-        5: [("C", 26)],
-        6: [("F", 23), ("F", 24), ("F", 25), ("F", 26)],
+        0: [("F", 7), ("F", 8), ("F", 9), ("F", 10), ("F", 11), ("X", 15), ("Y", 17)],
+        1: [("C", 14), ("C", 15), ("Y", 18)],
+        2: [("F", 12), ("F", 13), ("X", 19)],
+        3: [("C", 17)],
+        4: [("F", 14), ("F", 15), ("F", 16), ("F", 17), (1, 0)],
+        5: [("C", 19), (1, 1)],
+        6: [("F", 18), ("F", 19)],
         7: [(2, 0)],
     },
-    "ff_done": [(0, 3), (0, 4), (0, 5)],
-    "second_back": [("F", 6), (2, 1)],
-    "context_back": [(1, 3), (0, 6)],
+    "ff_done": [(2, 1), (0, 3), (0, 4), (0, 5)],
+    "second_back": [("F", 6)],
+    "context_back": [(3, 0), (2, 2), (1, 3), (0, 6)],
     "backward": {
-        0: [(3, 0), (2, 2), (1, 4)],
-        1: [(1, 5), (1, 6), (0, 7), (3, 1)],
-        2: [(3, 2), (2, 3), (1, 7)],
-        3: [(4, 0), (0, 8)],
-        4: [(4, 2), (2, 4), (1, 8)],
-        5: [(3, 3), (2, 5), (0, 9)],
-        6: [(2, 6), (2, 7), (1, 9)],
-        7: [(5, 0), (4, 1), (5, 2), (3, 4), (2, 8), (0, 10)],
-        8: [(6, 0), (5, 1), (6, 2), (4, 3), (3, 5), (1, 10)],
-        9: [(5, 3), (4, 4), (3, 6), (3, 7), (0, 11)],
-        10: [(6, 3), (5, 4), (4, 7), (3, 8), (2, 9), (1, 11)],
-        11: [(4, 5), (5, 7), (4, 8), (2, 10), (0, 12)],
+        0: [(1, 4)],
+        1: [(3, 1), (3, 2), (1, 5), (1, 6), (0, 7)],
+        2: [(4, 0), (2, 3), (1, 7)],
+        3: [(4, 1), (4, 2), (2, 4), (0, 8)],
+        4: [(5, 1), (3, 3), (1, 8)],
+        5: [(2, 5), (2, 7), (0, 9)],
+        6: [(3, 4), (2, 6), (2, 8), (1, 9)],
+        7: [(5, 0), (5, 2), (4, 3), (4, 4), (3, 5), (0, 10)],
+        8: [(6, 0), (6, 2), (5, 3), (5, 4), (3, 6), (3, 7), (1, 10), (2, 9)],
+        9: [(6, 3), (4, 7), (3, 8), (0, 11), (4, 5)],
+        10: [(4, 6), (5, 7), (4, 8), (2, 10), (1, 11), (5, 5)],
+        11: [(6, 5), (5, 6), (5, 8), (3, 9), (0, 12), (0, 13), (0, 14)],
     },
-    "attention_back": [],
+    "attention_back": [(2, 11)],
     "last": {
-        0: [(1, 12), (4, 6), (5, 8), (2, 11)],
-        1: [(5, 5), (3, 9)],
-        2: [(2, 12), (6, 5), (5, 6)],
-        3: [(4, 9), (3, 10)],
+        0: [(1, 12), (1, 13), (1, 14), (3, 10)],
+        1: [(2, 12), (6, 6), (4, 9)],
+        2: [(2, 13), (2, 14), (4, 10), (3, 11)],
+        3: [(5, 9), (3, 12)],
     },
-    "tail_one": [(6, 6), (5, 9), (3, 11)],
-    "tail_two": [(4, 10), (3, 12)],
-    "tail_three": [(4, 11), (5, 10), (4, 12), (5, 11), (5, 12)],
+    "tail_one": [(3, 13), (3, 14), (5, 10), (4, 11), (4, 12)],
+    "tail_two": [(4, 13), (4, 14)],
+    "tail_three": [(5, 11), (5, 12), (5, 13), (5, 14)],
 }
 
 
@@ -477,17 +466,18 @@
 
 
 class Reduce:
-    def __init__(self, place, ref, recv, first, second, third, res, sems, x_first):
+    def __init__(self, place, ref, recv, first, second, third, res, sems, x_first, start=0):
         self.p, self.ref, self.recv, self.first = place, ref, recv, first
         self.second, self.third, self.res, self.sems = second, third, res, sems
         self.x_first = x_first
         self.rows, self.half = recv.shape[2], recv.shape[3]
-        self.by_rows = ref.shape[2] > self.rows
+        self.by_rows, self.start = ref.shape[2] > self.rows, start
         self.steps = 6 if x_first else 5
 
     def share(self, core):
         if self.by_rows:
-            return pl.ds(aligned(core * self.rows, 16), self.rows), slice(None)
+            start = core * (self.ref.shape[2] // 2) + self.start
+            return pl.ds(aligned(start, 16), self.rows), slice(None)
         return slice(None), pl.ds(aligned(core * self.half, 128), self.half)
 
     def columns(self, core):
@@ -733,9 +723,17 @@
                 False,
             )
         )
+    take = iter(red_bufs)
+    results = []
     for i, (ref, _, x_first) in enumerate(grads):
-        recv, first, sec, third, res = red_bufs[5 * i : 5 * i + 5]
-        reds.append(Reduce(p, ref, recv, first, sec, third, res, red_sems.at[i], x_first))
+        res = next(take)
+        results.append(res)
+        parts = LAST_PARTS if i == len(grads) - 1 else 1
+        for k in range(parts):
+            bufs = [next(take) for _ in range(4)]
+            start = k * (rows // 2 // parts)
+            sems = red_sems.at[len(reds)]
+            reds.append(Reduce(p, ref, *bufs, res, sems, x_first, start))
 
     tokens_in = pltpu.make_async_copy(patches_ref, tokens, out_sems.at[0])
     tokens_in.start()
@@ -934,6 +932,12 @@
     big = 256
 
     def out_project(i, _):
+        for at, events in EVENTS["project"].items():
+
+            @pl.when(i == at)
+            def _(events=events):
+                go(*events)
+
         r = rows_of(i, big)
         m = tokens[r, :].astype(F32) + task_row()
         m = m + dot(context[:, r], w_out[0].reshape(width, width), 0, 0)
@@ -1185,7 +1189,7 @@
     ends[0].start()
     go(*EVENTS["tail_three"])
     for i, (_, done, _) in enumerate(grads):
-        copy = pltpu.make_async_copy(reds[i].res, done, out_sems.at[6 + i])
+        copy = pltpu.make_async_copy(results[i], done, out_sems.at[6 + i])
         copy.start()
         ends.append(copy)
     for copy in small_copies + member_copies + peer_copies:
@@ -1218,9 +1222,6 @@
     span = held_out.shape[0] // parts
     brought, copies = [], []
     middles = (from_in, from_gate, from_up, from_down)
-    for i, (source, middle) in enumerate(zip(sources[2:], middles)):
-        brought.append(pltpu.make_async_copy(source, middle, in_sems.at[i]))
-        brought[-1].start()
     whole = []
     for i in range(parts):
         r = pl.ds(i * span, span)
@@ -1233,6 +1234,9 @@
                 )
             )
             whole[-1][0].start()
+    for i, (source, middle) in enumerate(zip(sources[2:], middles)):
+        brought.append(pltpu.make_async_copy(source, middle, in_sems.at[i]))
+        brought[-1].start()
 
     def finish(i):
         copies.append(pltpu.make_async_copy(made[i], targets[2 + i], out_sems.at[12 + i]))
@@ -1247,6 +1251,7 @@
 
     brought[0].wait()
     for i in range(3):
+        pass_on(1)
         for g in range(groups):
             for core in range(2):
                 start = core * 384 + i * 128
@@ -1268,7 +1273,7 @@
     for j in range(2):
         made[6][j * half : (j + 1) * half, :] = from_down[j].astype(F32)
     finish(6)
-    pass_on(4)
+    pass_on(len(whole))
     one[...] = small[0, :rows]
     two[...] = small[1, :rows]
     table[...] = small[2 : 2 + held, :rows]
@@ -1287,27 +1292,21 @@
     groups = width // 256
     down_rows = w_down.shape[0] // 2
 
-    def of(rows, columns, x_first, by_rows=False):
-        whole = (rows, columns)
+    def of(rows, columns, x_first, row_parts=0):
         half = columns // 2
-        if by_rows:
-            rows, half = rows // 2, columns
-        if x_first:
-            shapes = [
-                (deep, 2, rows, half),
-                (deep, 2, rows // 2, half),
-                (deep, rows // 2, half),
-                (deep - 1, rows // 2, half),
-                whole,
-            ]
-        else:
-            shapes = [
-                (deep, 2, rows, half),
-                (deep, rows, half),
-                (deep - 1, rows, half),
-                (rows, half),
-                whole,
-            ]
+        shapes = [(rows, columns)]
+        if row_parts:
+            rows, half = rows // 2 // row_parts, columns
+        for _ in range(max(row_parts, 1)):
+            shapes.append((deep, 2, rows, half))
+            if x_first:
+                shapes.append((deep, 2, rows // 2, half))
+                shapes.append((deep, rows // 2, half))
+                shapes.append((deep - 1, rows // 2, half))
+            else:
+                shapes.append((deep, rows, half))
+                shapes.append((deep - 1, rows, half))
+                shapes.append((rows, half))
         return [pltpu.VMEM(shape, BF16) for shape in shapes]
 
     red_bufs = []
@@ -1316,8 +1315,8 @@
         red_bufs += of(rows, hidden // 2, False)
         red_bufs += of(down_rows, width, True)
     red_bufs += of(rows, width, True)
-    for _ in range(2 * groups):
-        red_bufs += of(rows, width // 2, False, True)
+    for pair in range(2 * groups):
+        red_bufs += of(rows, width // 2, False, LAST_PARTS if pair == 2 * groups - 1 else 1)
     sums = 7 + 2 * groups
     chunks = sum(PARTS)
     scratch = [
@@ -1349,7 +1348,7 @@
         pltpu.SemaphoreType.DMA((2, group - 1)),
         pltpu.SemaphoreType.DMA((2, reps - 1)),
         pltpu.SemaphoreType.DMA((2, group - 1)),
-        pltpu.SemaphoreType.DMA((sums, 2, deep + 4)),
+        pltpu.SemaphoreType.DMA((sums + LAST_PARTS - 1, 2, deep + 4)),
         pltpu.SemaphoreType.DMA((10 + sums,)),
         *red_bufs,
     ]

time: 197 us -> 191 us (0.970)
  Pallas kernels: 195 us -> 189 us
    pallas_call x1, Pallas kernels: 188 us -> 181 us  [fused(): pl.pallas_call(functools.partial(layer, config), out_shape=[shape((count,...]
where the time goes in v4:
time: 191 us
  Pallas kernels  189 us (99%)
  between operations  2.11 us (1%)
    pallas_call x1, Pallas kernels, fused(): pl.pallas_call(functools.partial(layer, config), out_shape=[shape((count,...  181 us
    pallas_call x1, Pallas kernels, fused(): pl.pallas_call(functools.partial(ending, (groups, group, rows, held)), ou...  7.28 us

profile of v4, /device:TPU:0, one launch (start us, length us, event | category | flops | bytes accessed | tf_op | source)
XLA Modules:
  0.0 190.8 jit_solution(4999172698249189053)
XLA Ops:
  1.9 181.5 %layer.1 = (bf16[1024,768]{1,0:T(8,128)(2,1)}, f32[1024,768]{1,0:T(8,128)}, bf16[4,96,768]{2,1,0:T(8,128)(2,1)}, bf16[2,96,1024]{2,1,0:T(8,128)(2,1)}, bf16[2,96...) custom-call(s32[1]{0:T(128)S(6)} %copy.26.refs_0_, ...), custom_call_target="tpu_custom_call" | custom-call | tf_op jit(solution)/shard_map/layer/pallas_call | solution.py:1359
  183.4 7.3 %ending.1 = (bf16[1,1024,768]{2,1,0:T(8,128)(2,1)}, f32[1,1024,768]{2,1,0:T(8,128)}, f32[96,768]{1,0:T(8,128)}, f32[96,768]{1,0:T(8,128)}, f32[96,768]{1,0:T(8,1...) custom-call(bf16[1024,768]{1,0:T(8,128)(2,1)} %get-tuple-element.31., ...), custom_call_target="tpu_custom_call" | custom-call | tf_op jit(solution)/shard_map/ending/pallas_call | solution.py:1384
